TPU v7x, 256 devices: a whole 4x4x8 slice. The times are simulated.
256 devices in a mesh: row: 64 (over y, z_hi, x), col: 4 (over z_lo, core).
Axes of the slice: x: 4, y: 4, z: 8 (z_hi: 4, z_lo: 2; z = z_hi * 2 + z_lo), core: 2. Of those that a mesh axis runs over, the one named last changes fastest.
Arguments:
- tile_values: bfloat16 [64, 4, 8, 512, 512], P('row', 'col'), may hold values from -0.25 to 0.25
- tile_coords: int32 [64, 4, 8, 2], P('row', 'col'), may hold values from 0 to 3, as said below
- tile_counts: int32 [64, 4], P('row', 'col'), may hold values from 1 to 8, as said below
- sketch: bfloat16 [4096, 1024], P('col'), may hold values from -6 to 6
Outputs:
- sketch_basis: float32 [4, 1024, 1024], P('col', 'row')
- triangle: float32 [1024, 1024], replicated
Inputs may be any that keep to these rules, and one draw needn't show every extreme that they name: `tile_coords`: entry [..., 0] is a tile row below 4 and entry [..., 1] a tile column below 2; the 8 positions in the list of one scenario block and column group are all distinct. `tile_counts`: some scenario block and column group has all 8 slots live.
All inputs are finite; a program needn't handle non-finite values.
Results may differ from a plain program's by a relative error of at most 0.00072.
Values may be sent and summed in bfloat16 or wider, within the bound.
No kernel may reach another device: no remote copies, remote signals or barrier semaphores. Data moves between devices by JAX's collectives and lax.ppermute only.
A program may use at most 128 MiB of HBM per device.

v0:
```python
import functools

import jax
import jax.numpy as jnp
from jax import lax
from jax.experimental import pallas as pl
from jax.experimental.pallas import tpu as pltpu
from jax.sharding import PartitionSpec as P

F32 = jnp.float32
BF16 = jnp.bfloat16
HI = lax.Precision.HIGHEST
TILE = 512
K = 1024
PARTS = 2
KW = K // PARTS
KH = KW // 2
NB = 128
shift_weight = 0.5

VMEM = pl.BlockSpec(memory_space=pltpu.VMEM)
SMEM = pl.BlockSpec(memory_space=pltpu.SMEM)


def call(body, outs, in_specs, args, scratch=(), limit=32, flops=0, moved=0):
    return pl.pallas_call(
        body,
        out_shape=tuple(jax.ShapeDtypeStruct(shape, dtype) for shape, dtype in outs),
        in_specs=in_specs,
        out_specs=tuple(VMEM for _ in outs),
        scratch_shapes=list(scratch),
        compiler_params=pltpu.CompilerParams(vmem_limit_bytes=limit << 20),
        cost_estimate=pl.CostEstimate(flops=flops, bytes_accessed=moved, transcendentals=0),
    )(*args)


PLANES = [[y * 16 + z * 4 + x for y in range(4) for x in range(4)] for z in range(4)]
COLUMNS = [[y * 16 + z * 4 + x for z in range(4)] for y in range(4) for x in range(4)]


def trade(value, groups):
    return lax.all_to_all(value, "row", 0, 0, tiled=True, axis_index_groups=groups)


def swap(value, bit):
    return lax.ppermute(value, "col", [(c, c ^ bit) for c in range(4)])


def swap_level(value, bit):
    return lax.ppermute(value, "row", [(r, r ^ (bit * 4)) for r in range(64)])


def find(places, count, i, j):
    slot, live = jnp.int32(0), jnp.int32(0)
    for s in range(8):
        match = (places[s, 0] == i) & (places[s, 1] == j) & (s < count)
        slot = jnp.where(match, s, slot)
        live = jnp.where(match, 1, live)
    return slot, live


def forward_body(first, places, count, tiles, sketch, *outs):
    me = lax.axis_index("col")
    for k in range(4):
        total = jnp.zeros((TILE, KW), F32)
        for j in range(2):
            slot, live = find(places, count[0, 0], me ^ k, j)
            strip = sketch[j * TILE:(j + 1) * TILE, first:first + KW]
            product = jnp.dot(tiles[slot], strip, preferred_element_type=F32)
            total = total + jnp.where(live > 0, product, 0.0)
        outs[k][...] = total


def forward(q, places, count, tiles, sketch):
    return call(
        functools.partial(forward_body, q * KW), [((TILE, KW), F32)] * 4, [SMEM, SMEM, VMEM, VMEM],
        (places, count, tiles, sketch), flops=16 * TILE * TILE * KW, moved=9 << 20,
    )


def backward_body(places, count, tiles, i0, i1, i2, i3, out):
    me = lax.axis_index("col")
    images = (i0, i1, i2, i3)
    for j in range(2):
        part = jnp.zeros((TILE, KW), F32)
        for k in range(4):
            slot, live = find(places, count[0, 0], me ^ k, j)
            product = lax.dot_general(
                tiles[slot], images[k][...], (((0,), (0,)), ((), ())), preferred_element_type=F32
            )
            part = part + jnp.where(live > 0, product, 0.0)
        for y in range(2):
            for z in range(4):
                for x in range(4):
                    start = y * 256 + z * 64 + x * 16
                    out[(2 * j + y) * 4 + x, z * 16:(z + 1) * 16, :] = part[start:start + 16, :]


def backward(places, count, tiles, images):
    return call(
        backward_body, [((16, 64, KW), F32)], [SMEM, SMEM] + [VMEM] * 5, (places, count, tiles, *images),
        flops=16 * TILE * TILE * KW, moved=8 << 20,
    )[0]


WIDE = 5 * NB


def strip_body(scale, rows_in, keep, give, rows, strip):
    for p in range(16):
        rows[p * 16:(p + 1) * 16, :K] = rows_in[p]
        rows[p * 16:(p + 1) * 16, K:] = rows_in[p, :, :WIDE]
    row = lax.axis_index("row")
    x = lax.rem(row, 4)
    start = pl.multiple_of(((row // 16) * 2 + x // 2) * NB, NB)
    strip[...] = scale * lax.dot_general(
        rows[:, pl.ds(start, NB)], rows[:, pl.ds(start, WIDE)], (((0,), (0,)), ((), ())),
        precision=HI, preferred_element_type=F32,
    )
    core = lax.rem(lax.axis_index("col"), 2)
    half = lax.rem(x, 2) * 64
    keep[...] = strip[pl.ds(pl.multiple_of(half + core * 32, 32), 32), :]
    give[...] = strip[pl.ds(pl.multiple_of(half + (1 - core) * 32, 32), 32), :]


def gram_parts(shifted, total_columns):
    rows = trade(jnp.broadcast_to(shifted[None], (16, *shifted.shape)), PLANES)
    keep, give = call(
        functools.partial(strip_body, 1.0 / total_columns), [((32, WIDE), F32)] * 2, [VMEM], (rows,),
        scratch=[pltpu.VMEM((256, K + WIDE), F32), pltpu.VMEM((NB, WIDE), F32)],
        flops=12 * 256 * NB * WIDE, moved=2 << 20,
    )
    total = keep + swap(give, 1)
    total = total + swap(total, 2)
    total = total + swap_level(total, 1)
    total = total + swap_level(total, 2)
    own = trade(jnp.broadcast_to(total[None], (16, *total.shape)), PLANES)
    return own, swap(own, 1)


def dot(a, b):
    return jnp.dot(a, b, precision=HI, preferred_element_type=F32)


def dot_tn(a, b):
    return lax.dot_general(a, b, (((0,), (0,)), ((), ())), precision=HI, preferred_element_type=F32)


def dot_nt(a, b):
    return lax.dot_general(a, b, (((1,), (1,)), ((), ())), precision=HI, preferred_element_type=F32)


def inverse_factor(block):
    groups = NB // 8
    sub = lax.broadcasted_iota(jnp.int32, (8, NB), 0)
    lane = lax.broadcasted_iota(jnp.int32, (8, NB), 1)
    w = [block[8 * g:8 * g + 8, :] for g in range(groups)]
    e = [jnp.where(lane == sub + 8 * g, 1.0, 0.0).astype(F32) for g in range(groups)]
    done = []
    for g in range(groups):
        z, ez = w[g], e[g]
        cols = [jnp.broadcast_to(z[:, 8 * g + k:8 * g + k + 1], (8, NB)) for k in range(8)]
        scale = jnp.zeros((8, NB), F32)
        kept = jnp.zeros((8, NB), F32)
        for k in range(8):
            here = sub == k
            pivot = jnp.broadcast_to(cols[k][k:k + 1, :], (8, NB))
            r = 1.0 / pivot
            zrow = jnp.broadcast_to(z[k:k + 1, :], (8, NB))
            erow = jnp.broadcast_to(ez[k:k + 1, :], (8, NB))
            scale = jnp.where(here, lax.rsqrt(pivot), scale)
            kept = jnp.where(here, erow, kept)
            t = jnp.where(here, 1.0 - r, cols[k] * r)
            z = z - t * zrow
            ez = ez - t * erow
            for l in range(k + 1, 8):
                cols[l] = cols[l] - t * jnp.broadcast_to(cols[l][k:k + 1, :], (8, NB))
        done.append(kept * scale)
        if g + 1 < groups:
            zrows = [jnp.broadcast_to(z[k:k + 1, :], (8, NB)) for k in range(8)]
            erows = [jnp.broadcast_to(ez[k:k + 1, :], (8, NB)) for k in range(8)]
            for i in range(g + 1, groups):
                acc, eacc = w[i], e[i]
                for k in range(8):
                    c = jnp.broadcast_to(w[i][:, 8 * g + k:8 * g + k + 1], (8, NB))
                    acc = acc - c * zrows[k]
                    eacc = eacc - c * erows[k]
                w[i], e[i] = acc, eacc
    return jnp.concatenate(done, axis=0)


def factor_body(own, other, shifted, basis, triangle, work, inv):
    core = lax.rem(lax.axis_index("col"), 2)
    for p in range(16):
        for held, half in ((own, core), (other, 1 - core)):
            here = pl.ds(pl.multiple_of(p * 64 + half * 32, 32), 32)
            for d in range(5):
                block = (p // 2 + d) % 8
                work[here, block * NB:(block + 1) * NB] = held[p, :, d * NB:(d + 1) * NB]
    for i in range(3):
        for j in range(i + 5, 8):
            low = work[j * NB:(j + 1) * NB, i * NB:(i + 1) * NB]
            work[i * NB:(i + 1) * NB, j * NB:(j + 1) * NB] = low.T
    basis[...] = shifted[...]
    rows = lax.broadcasted_iota(jnp.int32, (NB, K), 0)
    lanes = lax.broadcasted_iota(jnp.int32, (NB, K), 1)

    def panel(j, _):
        offset = pl.multiple_of(j * NB, NB)
        here = pl.ds(offset, NB)
        inv[...] = inverse_factor(work[here, here])
        row = dot(inv[...], work[here, :])
        row = jnp.where(lanes >= rows + offset, row, 0.0)
        triangle[here, :] = row
        own = dot_nt(basis[:, here], inv[...])
        basis[...] = basis[...] - dot(own, row)
        basis[:, here] = own

        def trail(k, _):
            there = pl.ds(pl.multiple_of(k * NB, NB), NB)
            work[there, :] = work[there, :] - dot_tn(triangle[here, there], triangle[here, :])
            return 0

        lax.fori_loop(j + 1, K // NB, trail, 0)
        return 0

    lax.fori_loop(0, K // NB, panel, 0)


def local(tile_values, tile_coords, tile_counts, sketch):
    tiles, places = tile_values[0, 0], tile_coords[0, 0]
    partial = [forward(q, places, tile_counts, tiles, sketch) for q in range(PARTS)]
    paired = [(p[0] + swap(p[1], 1), p[2] + swap(p[3], 1)) for p in partial]
    summed, image = [], None
    for own, other in paired:
        if image is not None:
            other, image = lax.optimization_barrier((other, image))
        image = (own + swap(other, 2)).astype(BF16)
        across = swap(image, 2)
        four = (image, swap(image, 1), across, swap(across, 1))
        summed.append(jnp.sum(trade(backward(places, tile_counts, tiles, four), PLANES), axis=0))
    summed = jnp.concatenate(summed, axis=1)
    summed = jnp.sum(trade(summed.reshape(4, 16, K), COLUMNS), axis=0)
    own_count = summed.shape[0]
    offset = lax.axis_index("row") * own_count
    shifted = summed + shift_weight * lax.dynamic_slice_in_dim(sketch, offset, own_count, 0).astype(F32)
    own, other = gram_parts(shifted, sketch.shape[0] * 4)
    basis, triangle = call(
        factor_body, [((16, K), F32), ((K, K), F32)], [VMEM] * 3, (own, other, shifted),
        scratch=[pltpu.VMEM((K, K), F32), pltpu.VMEM((NB, NB), F32)], limit=40,
        flops=4 * K * K * K, moved=8 << 20,
    )
    return (basis[None], triangle)


def solution(mesh):
    in_specs = (
        P("row", "col", None, None, None),
        P("row", "col", None, None),
        P("row", "col"),
        P("col", None),
    )
    out_specs = (P("col", "row", None), P())
    return jax.shard_map(local, mesh=mesh, in_specs=in_specs, out_specs=out_specs, check_vma=False)
```

profile of v0, /device:TPU:1, one launch (start us, length us, event | category | flops | bytes accessed | tf_op | source)
XLA Modules:
  0.0 291.1 jit_solution(12943035362239030294)
XLA Ops:
  0.6 0.8 copy.11.places
  2.0 2.2 copy-done
  4.2 1.6 copy-done.2
  5.8 3.0 %shard_map.59 = (f32[512,512]{1,0:T(8,128)S(1)}, f32[512,512]{1,0:T(8,128)S(1)}, f32[512,512]{1,0:T(8,128)S(1)}, f32[512,512]{1,0:T(8,128)S(1)}) custom-call(s32[8,2]{1,0:T(8,128)S(1)} %copy.11.places, s32[1,1]{1,0:T(1,128)S(6)} %copy.14.count, bf16[8,512,512]{2,1,0:T(8,128)(2,1)S(1)} %bitcast.4, bf16[1024,1024]{1,0:T(8,128)(2,1)S(1)} %copy-done.2), custom_call_target="tpu_custom_call" | custom-call | flops 2147483648 | bytes 9437184 | tf_op jit(solution)/shard_map/pallas_call | solution.py:26
  8.8 3.3 %collective-permute-start.1 = (f32[512,512]{1,0:T(8,128)S(1)}, f32[512,512]{1,0:T(8,128)S(1)}, u32[]{:S(2)}, u32[]{:S(2)}) collective-permute-start(f32[512,512]{1,0:T(8,128)S(1)} %get-tuple-element.18), channel_id=1, source_target_pairs={{0,1},{1,0},{2,3},{3,2},{4,5},{5,4},{6,7},{7,6},{8,9},{9,8},{10,11... | collective-permute-start | bytes 3145736 | tf_op jit(solution)/shard_map/ppermute | solution.py:46
  12.2 2.2 collective-permute-done.1
  14.4 0.2 add.37
  14.7 3.0 %shard_map.61 = (f32[512,512]{1,0:T(8,128)S(1)}, f32[512,512]{1,0:T(8,128)S(1)}, f32[512,512]{1,0:T(8,128)S(1)}, f32[512,512]{1,0:T(8,128)S(1)}) custom-call(s32[8,2]{1,0:T(8,128)S(1)} %copy.11.places, s32[1,1]{1,0:T(1,128)S(6)} %copy.14.count, bf16[8,512,512]{2,1,0:T(8,128)(2,1)S(1)} %bitcast.5, bf16[1024,1024]{1,0:T(8,128)(2,1)S(1)} %copy-done.2), custom_call_target="tpu_custom_call" | custom-call | flops 2147483648 | bytes 9437184 | tf_op jit(solution)/shard_map/pallas_call | solution.py:26
  17.7 0.6 collective-permute-start.7
  18.4 20.7 %collective-permute-done.2 = f32[512,512]{1,0:T(8,128)S(1)} collective-permute-done((f32[512,512]{1,0:T(8,128)S(1)}, f32[512,512]{1,0:T(8,128)S(1)}, u32[]{:S(2)}, u32[]{:S(2)}) %collective-permute-start.2) | collective-permute-done | bytes 1048608 | tf_op jit(solution)/shard_map/ppermute | solution.py:46
  39.1 0.4 add_convert_fusion.1.i0
  39.5 0.2 collective-permute-start.4
  39.7 1.4 collective-permute-start.3
  41.1 10.7 %collective-permute-done.4.i2 = bf16[512,512]{1,0:T(8,128)(2,1)S(1)} collective-permute-done((bf16[512,512]{1,0:T(8,128)(2,1)S(1)}, bf16[512,512]{1,0:T(8,128)(2,1)S(1)}, u32[]{:S(2)}, u32[]{:S(2)}) %collective-permute-start.4) | collective-permute-done | bytes 524320 | tf_op jit(solution)/shard_map/ppermute | solution.py:46
  51.8 2.1 collective-permute-start.5
  53.9 1.2 add.40
  55.2 0.2 collective-permute-done.5.i3
  55.5 4.4 %shard_map.60 = f32[16,64,512]{2,1,0:T(8,128)} custom-call(s32[8,2]{1,0:T(8,128)S(1)} %copy.11.places, s32[1,1]{1,0:T(1,128)S(6)} %copy.14.count, bf16[8,512,512]{2,1,0:T(8,128)(2,1)S(1)} %bitcast.6, bf16[512,512]{1,0:T(8,128)(2,1)S(1)} %add_convert_fusion.1.i0, bf16[512,512]{1,0:T(8,128)(2,1)S(1)} %collective-permute-done.3.i1, ...), custom_call_target="tpu_custom_call" | custom-call | flops 2147483648 | bytes 8388608 | tf_op jit(solution)/shard_map/pallas_call | solution.py:26
  59.9 6.4 %all-to-all-start = ((f32[16,64,512]{2,1,0:T(8,128)}), f32[16,64,512]{2,1,0:T(8,128)}, u32[]{:S(2)}, u32[]{:S(2)}) async-start(f32[16,64,512]{2,1,0:T(8,128)} %shard_map.60), calls=%async_computation | async-start | bytes 4194304 | tf_op jit(solution)/shard_map/all_to_all | solution.py:42
  66.3 13.4 %collective-permute-done.8 = f32[512,512]{1,0:T(8,128)} collective-permute-done((f32[512,512]{1,0:T(8,128)}, f32[512,512]{1,0:T(8,128)}, u32[]{:S(2)}, u32[]{:S(2)}) %collective-permute-start.8) | collective-permute-done | bytes 1048608 | tf_op jit(solution)/shard_map/ppermute | solution.py:46
  79.6 1.5 add_convert_fusion.i0
  81.4 1.6 collective-permute-start.9
  83.0 10.4 %collective-permute-done.10.i2 = bf16[512,512]{1,0:T(8,128)(2,1)S(1)} collective-permute-done((bf16[512,512]{1,0:T(8,128)(2,1)S(1)}, bf16[512,512]{1,0:T(8,128)(2,1)S(1)}, u32[]{:S(2)}, u32[]{:S(2)}) %collective-permute-start.10) | collective-permute-done | bytes 524320 | tf_op jit(solution)/shard_map/ppermute | solution.py:46
  93.4 2.2 collective-permute-start.11
  95.6 1.5 collective-permute-done.11.i3
  97.1 2.2 copy-done.1
  99.3 4.4 %shard_map.62 = f32[16,64,512]{2,1,0:T(8,128)} custom-call(s32[8,2]{1,0:T(8,128)S(1)} %copy.11.places, s32[1,1]{1,0:T(1,128)S(6)} %copy.14.count, bf16[8,512,512]{2,1,0:T(8,128)(2,1)S(1)} %bitcast.7, bf16[512,512]{1,0:T(8,128)(2,1)S(1)} %add_convert_fusion.i0, bf16[512,512]{1,0:T(8,128)(2,1)S(1)} %collective-permute-done.9.i1, ...), custom_call_target="tpu_custom_call" | custom-call | flops 2147483648 | bytes 8388608 | tf_op jit(solution)/shard_map/pallas_call | solution.py:26
  103.7 5.4 %all-to-all-start.1 = ((f32[16,64,512]{2,1,0:T(8,128)}), f32[16,64,512]{2,1,0:T(8,128)S(1)}, u32[]{:S(2)}, u32[]{:S(2)}) async-start(f32[16,64,512]{2,1,0:T(8,128)} %shard_map.62), calls=%async_computation.1 | async-start | bytes 4194304 | tf_op jit(solution)/shard_map/all_to_all | solution.py:42
  109.1 1.8 reduce_sum.27
  110.9 30.3 %all-to-all-done.1 = f32[16,64,512]{2,1,0:T(8,128)S(1)} async-done(((f32[16,64,512]{2,1,0:T(8,128)}), f32[16,64,512]{2,1,0:T(8,128)S(1)}, u32[]{:S(2)}, u32[]{:S(2)}) %all-to-all-start.1) | async-done | bytes 2097184 | tf_op jit(solution)/shard_map/all_to_all | solution.py:42
  141.3 0.7 pad_maximum_fusion
  142.0 7.8 %all-to-all-start.2 = ((f32[4,16,1024]{2,1,0:T(8,128)}), f32[4,16,1024]{2,1,0:T(8,128)S(1)}, u32[]{:S(2)}, u32[]{:S(2)}) async-start(f32[4,16,1024]{2,1,0:T(8,128)} %bitcast.2), calls=%async_computation.2 | async-start | bytes 524288 | tf_op jit(solution)/shard_map/all_to_all | solution.py:42
  149.9 8.2 %all-to-all-done.2 = f32[4,16,1024]{2,1,0:T(8,128)S(1)} async-done(((f32[4,16,1024]{2,1,0:T(8,128)}), f32[4,16,1024]{2,1,0:T(8,128)S(1)}, u32[]{:S(2)}, u32[]{:S(2)}) %all-to-all-start.2) | async-done | bytes 262176 | tf_op jit(solution)/shard_map/all_to_all | solution.py:42
  158.0 0.8 multiply_add_fusion.shifted
  158.9 17.1 %all_to_all.25.rows_in = f32[16,16,1024]{2,1,0:T(8,128)S(1)} all-to-all(f32[16,16,1024]{2,1,0:T(8,128)S(1)} %broadcast_in_dim.6), channel_id=1, replica_groups={{0,4,8,12,64,68,72,76,128,132,136,140,192,196,200,204},{16,20,24,28,80,..., dimensions={0} | all-to-all | bytes 2097152 | tf_op jit(solution)/shard_map/all_to_all | solution.py:42
  176.0 0.6 shard_map.63
  176.6 4.7 %collective-permute-start.12 = (f32[32,640]{1,0:T(8,128)S(1)}, f32[32,640]{1,0:T(8,128)S(1)}, u32[]{:S(2)}, u32[]{:S(2)}) collective-permute-start(f32[32,640]{1,0:T(8,128)S(1)} %get-tuple-element.25), channel_id=1, source_target_pairs={{0,1},{1,0},{2,3},{3,2},{4,5},{5,4},{6,7},{7,6},{8,9},{9,8},{10,11... | collective-permute-start | bytes 245768 | tf_op jit(solution)/shard_map/ppermute | solution.py:46
  181.3 0.9 collective-permute-done.12
  182.2 1.3 collective-permute-start.13
  183.5 2.5 collective-permute-done.13
  186.0 2.3 collective-permute-start.14
  188.3 2.0 collective-permute-done.14
  190.3 4.9 %collective-permute-start.15 = (f32[32,640]{1,0:T(8,128)S(1)}, f32[32,640]{1,0:T(8,128)S(1)}, u32[]{:S(2)}, u32[]{:S(2)}) collective-permute-start(f32[32,640]{1,0:T(8,128)S(1)} %add.46), channel_id=1, source_target_pairs={{0,32},{4,36},{8,40},{12,44},{16,48},{20,52},{24,56},{28,60},{32,0... | collective-permute-start | bytes 245768 | tf_op jit(solution)/shard_map/ppermute | solution.py:50
  195.2 2.4 collective-permute-done.15
  197.8 17.9 %all_to_all.26.own = f32[16,32,640]{2,1,0:T(8,128)S(1)} all-to-all(f32[16,32,640]{2,1,0:T(8,128)S(1)} %broadcast_in_dim.7), channel_id=1, replica_groups={{0,4,8,12,64,68,72,76,128,132,136,140,192,196,200,204},{16,20,24,28,80,..., dimensions={0} | all-to-all | bytes 2621440 | tf_op jit(solution)/shard_map/all_to_all | solution.py:42
  215.7 5.8 %collective-permute-start.16 = (f32[16,32,640]{2,1,0:T(8,128)S(1)}, f32[16,32,640]{2,1,0:T(8,128)S(1)}, u32[]{:S(2)}, u32[]{:S(2)}) collective-permute-start(f32[16,32,640]{2,1,0:T(8,128)S(1)} %all_to_all.26.own), channel_id=1, source_target_pairs={{0,1},{1,0},{2,3},{3,2},{4,5},{5,4},{6,7},{7,6},{8,9},{9,8},{10,11... | collective-permute-start | bytes 3932168 | tf_op jit(solution)/shard_map/ppermute | solution.py:46
  221.5 2.7 collective-permute-done.16.other
  224.1 67.0 %shard_map.64 = (f32[16,1024]{1,0:T(8,128)}, f32[1024,1024]{1,0:T(8,128)}) custom-call(f32[16,32,640]{2,1,0:T(8,128)S(1)} %all_to_all.26.own, f32[16,32,640]{2,1,0:T(8,128)S(1)} %collective-permute-done.16.other, f32[16,1024]{1,0:T(8,128)S(1)} %multiply_add_fusion.shifted), custom_call_target="tpu_custom_call" | custom-call | flops 4294967296 | bytes 8388608 | tf_op jit(solution)/shard_map/pallas_call | solution.py:26
  (22 shorter events, 1.0 us)
Async XLA Ops:
  2.0 2.2 copy-start
  4.2 1.6 copy-start.2
  8.8 5.6 %collective-permute-start.1 = (f32[512,512]{1,0:T(8,128)S(1)}, f32[512,512]{1,0:T(8,128)S(1)}, u32[]{:S(2)}, u32[]{:S(2)}) collective-permute-start(f32[512,512]{1,0:T(8,128)S(1)} %get-tuple-element.18), channel_id=1, source_target_pairs={{0,1},{1,0},{2,3},{3,2},{4,5},{5,4},{6,7},{7,6},{8,9},{9,8},{10,11... | collective-permute-start | bytes 3145736 | tf_op jit(solution)/shard_map/ppermute | solution.py:46
  12.1 6.2 %collective-permute-start = (f32[512,512]{1,0:T(8,128)S(1)}, f32[512,512]{1,0:T(8,128)S(1)}, u32[]{:S(2)}, u32[]{:S(2)}) collective-permute-start(f32[512,512]{1,0:T(8,128)S(1)} %get-tuple-element.16), channel_id=1, source_target_pairs={{0,1},{1,0},{2,3},{3,2},{4,5},{5,4},{6,7},{7,6},{8,9},{9,8},{10,11... | collective-permute-start | bytes 3145736 | tf_op jit(solution)/shard_map/ppermute | solution.py:46
  14.6 24.5 %collective-permute-start.2 = (f32[512,512]{1,0:T(8,128)S(1)}, f32[512,512]{1,0:T(8,128)S(1)}, u32[]{:S(2)}, u32[]{:S(2)}) collective-permute-start(f32[512,512]{1,0:T(8,128)S(1)} %add.37), channel_id=1, source_target_pairs={{0,2},{1,3},{2,0},{3,1},{4,6},{5,7},{6,4},{7,5},{8,10},{9,11},{10,... | collective-permute-start | bytes 3145736 | tf_op jit(solution)/shard_map/ppermute | solution.py:46
  17.7 36.2 %collective-permute-start.7 = (f32[512,512]{1,0:T(8,128)S(1)}, f32[512,512]{1,0:T(8,128)S(1)}, u32[]{:S(2)}, u32[]{:S(2)}) collective-permute-start(f32[512,512]{1,0:T(8,128)S(1)} %get-tuple-element.22), channel_id=1, source_target_pairs={{0,1},{1,0},{2,3},{3,2},{4,5},{5,4},{6,7},{7,6},{8,9},{9,8},{10,11... | collective-permute-start | bytes 3145736 | tf_op jit(solution)/shard_map/ppermute | solution.py:46
  39.5 12.3 %collective-permute-start.4 = (bf16[512,512]{1,0:T(8,128)(2,1)S(1)}, bf16[512,512]{1,0:T(8,128)(2,1)S(1)}, u32[]{:S(2)}, u32[]{:S(2)}) collective-permute-start(bf16[512,512]{1,0:T(8,128)(2,1)S(1)} %add_convert_fusion.1.i0), channel_id=1, source_target_pairs={{0,2},{1,3},{2,0},{3,1},{4,6},{5,7},{6,4},{7,5},{8,10},{9,11},{10,... | collective-permute-start | bytes 1572872 | tf_op jit(solution)/shard_map/ppermute | solution.py:46
  39.7 15.5 %collective-permute-start.3 = (bf16[512,512]{1,0:T(8,128)(2,1)S(1)}, bf16[512,512]{1,0:T(8,128)(2,1)S(1)}, u32[]{:S(2)}, u32[]{:S(2)}) collective-permute-start(bf16[512,512]{1,0:T(8,128)(2,1)S(1)} %add_convert_fusion.1.i0), channel_id=1, source_target_pairs={{0,1},{1,0},{2,3},{3,2},{4,5},{5,4},{6,7},{7,6},{8,9},{9,8},{10,11... | collective-permute-start | bytes 1572872 | tf_op jit(solution)/shard_map/ppermute | solution.py:46
  51.8 3.7 %collective-permute-start.5 = (bf16[512,512]{1,0:T(8,128)(2,1)S(1)}, bf16[512,512]{1,0:T(8,128)(2,1)S(1)}, u32[]{:S(2)}, u32[]{:S(2)}) collective-permute-start(bf16[512,512]{1,0:T(8,128)(2,1)S(1)} %collective-permute-done.4.i2), channel_id=1, source_target_pairs={{0,1},{1,0},{2,3},{3,2},{4,5},{5,4},{6,7},{7,6},{8,9},{9,8},{10,11... | collective-permute-start | bytes 1572872 | tf_op jit(solution)/shard_map/ppermute | solution.py:46
  53.9 12.3 %collective-permute-start.6 = (f32[512,512]{1,0:T(8,128)S(1)}, f32[512,512]{1,0:T(8,128)S(1)}, u32[]{:S(2)}, u32[]{:S(2)}) collective-permute-start(f32[512,512]{1,0:T(8,128)S(1)} %get-tuple-element.20), channel_id=1, source_target_pairs={{0,1},{1,0},{2,3},{3,2},{4,5},{5,4},{6,7},{7,6},{8,9},{9,8},{10,11... | collective-permute-start | bytes 3145736 | tf_op jit(solution)/shard_map/ppermute | solution.py:46
  55.1 24.5 %collective-permute-start.8 = (f32[512,512]{1,0:T(8,128)}, f32[512,512]{1,0:T(8,128)}, u32[]{:S(2)}, u32[]{:S(2)}) collective-permute-start(f32[512,512]{1,0:T(8,128)} %add.40), channel_id=1, source_target_pairs={{0,2},{1,3},{2,0},{3,1},{4,6},{5,7},{6,4},{7,5},{8,10},{9,11},{10,... | collective-permute-start | bytes 3145736 | tf_op jit(solution)/shard_map/ppermute | solution.py:46
  59.9 43.9 %all-to-all-start = ((f32[16,64,512]{2,1,0:T(8,128)}), f32[16,64,512]{2,1,0:T(8,128)}, u32[]{:S(2)}, u32[]{:S(2)}) async-start(f32[16,64,512]{2,1,0:T(8,128)} %shard_map.60), calls=%async_computation | async-start | bytes 4194304 | tf_op jit(solution)/shard_map/all_to_all | solution.py:42
  81.2 12.2 %collective-permute-start.10 = (bf16[512,512]{1,0:T(8,128)(2,1)S(1)}, bf16[512,512]{1,0:T(8,128)(2,1)S(1)}, u32[]{:S(2)}, u32[]{:S(2)}) collective-permute-start(bf16[512,512]{1,0:T(8,128)(2,1)S(1)} %add_convert_fusion.i0), channel_id=1, source_target_pairs={{0,2},{1,3},{2,0},{3,1},{4,6},{5,7},{6,4},{7,5},{8,10},{9,11},{10,... | collective-permute-start | bytes 1572872 | tf_op jit(solution)/shard_map/ppermute | solution.py:46
  81.4 14.2 %collective-permute-start.9 = (bf16[512,512]{1,0:T(8,128)(2,1)S(1)}, bf16[512,512]{1,0:T(8,128)(2,1)S(1)}, u32[]{:S(2)}, u32[]{:S(2)}) collective-permute-start(bf16[512,512]{1,0:T(8,128)(2,1)S(1)} %add_convert_fusion.i0), channel_id=1, source_target_pairs={{0,1},{1,0},{2,3},{3,2},{4,5},{5,4},{6,7},{7,6},{8,9},{9,8},{10,11... | collective-permute-start | bytes 1572872 | tf_op jit(solution)/shard_map/ppermute | solution.py:46
  93.4 3.7 %collective-permute-start.11 = (bf16[512,512]{1,0:T(8,128)(2,1)S(1)}, bf16[512,512]{1,0:T(8,128)(2,1)S(1)}, u32[]{:S(2)}, u32[]{:S(2)}) collective-permute-start(bf16[512,512]{1,0:T(8,128)(2,1)S(1)} %collective-permute-done.10.i2), channel_id=1, source_target_pairs={{0,1},{1,0},{2,3},{3,2},{4,5},{5,4},{6,7},{7,6},{8,9},{9,8},{10,11... | collective-permute-start | bytes 1572872 | tf_op jit(solution)/shard_map/ppermute | solution.py:46
  97.1 2.2 copy-start.1
  103.7 37.4 %all-to-all-start.1 = ((f32[16,64,512]{2,1,0:T(8,128)}), f32[16,64,512]{2,1,0:T(8,128)S(1)}, u32[]{:S(2)}, u32[]{:S(2)}) async-start(f32[16,64,512]{2,1,0:T(8,128)} %shard_map.62), calls=%async_computation.1 | async-start | bytes 4194304 | tf_op jit(solution)/shard_map/all_to_all | solution.py:42
  142.0 16.0 %all-to-all-start.2 = ((f32[4,16,1024]{2,1,0:T(8,128)}), f32[4,16,1024]{2,1,0:T(8,128)S(1)}, u32[]{:S(2)}, u32[]{:S(2)}) async-start(f32[4,16,1024]{2,1,0:T(8,128)} %bitcast.2), calls=%async_computation.2 | async-start | bytes 524288 | tf_op jit(solution)/shard_map/all_to_all | solution.py:42
  176.6 5.6 %collective-permute-start.12 = (f32[32,640]{1,0:T(8,128)S(1)}, f32[32,640]{1,0:T(8,128)S(1)}, u32[]{:S(2)}, u32[]{:S(2)}) collective-permute-start(f32[32,640]{1,0:T(8,128)S(1)} %get-tuple-element.25), channel_id=1, source_target_pairs={{0,1},{1,0},{2,3},{3,2},{4,5},{5,4},{6,7},{7,6},{8,9},{9,8},{10,11... | collective-permute-start | bytes 245768 | tf_op jit(solution)/shard_map/ppermute | solution.py:46
  182.2 3.8 %collective-permute-start.13 = (f32[32,640]{1,0:T(8,128)S(1)}, f32[32,640]{1,0:T(8,128)S(1)}, u32[]{:S(2)}, u32[]{:S(2)}) collective-permute-start(f32[32,640]{1,0:T(8,128)S(1)} %add.44), channel_id=1, source_target_pairs={{0,2},{1,3},{2,0},{3,1},{4,6},{5,7},{6,4},{7,5},{8,10},{9,11},{10,... | collective-permute-start | bytes 245768 | tf_op jit(solution)/shard_map/ppermute | solution.py:46
  186.0 4.3 %collective-permute-start.14 = (f32[32,640]{1,0:T(8,128)S(1)}, f32[32,640]{1,0:T(8,128)S(1)}, u32[]{:S(2)}, u32[]{:S(2)}) collective-permute-start(f32[32,640]{1,0:T(8,128)S(1)} %add.45), channel_id=1, source_target_pairs={{0,16},{4,20},{8,24},{12,28},{16,0},{20,4},{24,8},{28,12},{32,48},... | collective-permute-start | bytes 245768 | tf_op jit(solution)/shard_map/ppermute | solution.py:50
  190.3 7.4 %collective-permute-start.15 = (f32[32,640]{1,0:T(8,128)S(1)}, f32[32,640]{1,0:T(8,128)S(1)}, u32[]{:S(2)}, u32[]{:S(2)}) collective-permute-start(f32[32,640]{1,0:T(8,128)S(1)} %add.46), channel_id=1, source_target_pairs={{0,32},{4,36},{8,40},{12,44},{16,48},{20,52},{24,56},{28,60},{32,0... | collective-permute-start | bytes 245768 | tf_op jit(solution)/shard_map/ppermute | solution.py:50
  215.7 8.4 %collective-permute-start.16 = (f32[16,32,640]{2,1,0:T(8,128)S(1)}, f32[16,32,640]{2,1,0:T(8,128)S(1)}, u32[]{:S(2)}, u32[]{:S(2)}) collective-permute-start(f32[16,32,640]{2,1,0:T(8,128)S(1)} %all_to_all.26.own), channel_id=1, source_target_pairs={{0,1},{1,0},{2,3},{3,2},{4,5},{5,4},{6,7},{7,6},{8,9},{9,8},{10,11... | collective-permute-start | bytes 3932168 | tf_op jit(solution)/shard_map/ppermute | solution.py:46
where the time goes:
time: 293 us; the launch traced here: 291 us
  waiting for transfers between devices  108 us (37%)
  Pallas kernels  82.4 us (28%)
  starting transfers between devices  50.5 us (17%)
  blocking collectives  35 us (12%)
  local copies, waits for them, and re-layouts  6.94 us (2%)
  other arithmetic  6.79 us (2%)
    pallas_call x6, Pallas kernels, call(): pl.pallas_call(body, out_shape=tuple((jax.ShapeDtypeStruct(shape, dtype)...  82.4 us
    ppermute x15, waiting for transfers between devices, swap(): return lax.ppermute(value, 'col', [(c, c ^ bit) for c in range(4)])  65.3 us
    all_to_all x3, waiting for transfers between devices, trade(): lax.all_to_all(value, 'row', 0, 0, tiled=True, axis_index_groups=groups)  38.4 us
    all_to_all x2, blocking collectives, trade(): lax.all_to_all(value, 'row', 0, 0, tiled=True, axis_index_groups=groups)  35 us
    ppermute x15, starting transfers between devices, swap(): return lax.ppermute(value, 'col', [(c, c ^ bit) for c in range(4)])  23.7 us
    all_to_all x3, starting transfers between devices, trade(): lax.all_to_all(value, 'row', 0, 0, tiled=True, axis_index_groups=groups)  19.6 us
    ppermute x2, starting transfers between devices, swap_level(): return lax.ppermute(value, 'row', [(r, r ^ bit * 4) for r in range(64)])  7.23 us
    unnamed x6, local copies, waits for them, and re-layouts  5.96 us
  transfers between devices with their start and end apart: 20, of which 14 were waited for; matrix products, arithmetic and copies ran while one was open for 2% of the time, Pallas kernels for 4%

commit v1 on v0

--- a/solution.py
+++ b/solution.py
@@ -20,6 +20,7 @@
 
 VMEM = pl.BlockSpec(memory_space=pltpu.VMEM)
 SMEM = pl.BlockSpec(memory_space=pltpu.SMEM)
+HBM = pl.BlockSpec(memory_space=pltpu.HBM)
 
 
 def call(body, outs, in_specs, args, scratch=(), limit=32, flops=0, moved=0):
@@ -59,36 +60,53 @@
     return slot, live
 
 
-def forward_body(first, places, count, tiles, sketch, *outs):
-    me = lax.axis_index("col")
-    for k in range(4):
+def start_tiles(order, places, count, tiles, held, sems):
+    copies, lives = {}, {}
+    for n, (k, j) in enumerate(order):
+        slot, lives[k, j] = find(places, count[0, 0], lax.axis_index("col") ^ k, j)
+        copies[k, j] = pltpu.make_async_copy(tiles.at[slot], held.at[n], sems.at[n])
+        copies[k, j].start()
+    return copies, lives
+
+
+def forward_body(first, places, count, tiles, sketch, o0, o1, o2, o3, held, strip, sems):
+    outs = (o0, o1, o2, o3)
+    order = [(k, j) for k in (1, 3, 0, 2) for j in range(2)]
+    load = pltpu.make_async_copy(sketch.at[:, pl.ds(first, KW)], strip, sems.at[8])
+    load.start()
+    copies, lives = start_tiles(order, places, count, tiles, held, sems)
+    load.wait()
+    for k in (1, 3, 0, 2):
         total = jnp.zeros((TILE, KW), F32)
         for j in range(2):
-            slot, live = find(places, count[0, 0], me ^ k, j)
-            strip = sketch[j * TILE:(j + 1) * TILE, first:first + KW]
-            product = jnp.dot(tiles[slot], strip, preferred_element_type=F32)
-            total = total + jnp.where(live > 0, product, 0.0)
+            copies[k, j].wait()
+            tile = held[order.index((k, j))]
+            product = jnp.dot(tile, strip[j * TILE:(j + 1) * TILE, :], preferred_element_type=F32)
+            total = total + jnp.where(lives[k, j] > 0, product, 0.0)
         outs[k][...] = total
 
 
 def forward(q, places, count, tiles, sketch):
     return call(
-        functools.partial(forward_body, q * KW), [((TILE, KW), F32)] * 4, [SMEM, SMEM, VMEM, VMEM],
-        (places, count, tiles, sketch), flops=16 * TILE * TILE * KW, moved=9 << 20,
-    )
-
-
-def backward_body(places, count, tiles, i0, i1, i2, i3, out):
-    me = lax.axis_index("col")
+        functools.partial(forward_body, q * KW), [((TILE, KW), F32)] * 4, [SMEM, SMEM, HBM, HBM],
+        (places, count, tiles, sketch),
+        scratch=[pltpu.VMEM((8, TILE, TILE), BF16), pltpu.VMEM((2 * TILE, KW), BF16), pltpu.SemaphoreType.DMA((9,))],
+        limit=20, flops=16 * TILE * TILE * KW, moved=9 << 20,
+    )
+
+
+def backward_body(places, count, tiles, i0, i1, i2, i3, out, held, sems):
     images = (i0, i1, i2, i3)
+    order = [(k, j) for j in range(2) for k in range(4)]
+    copies, lives = start_tiles(order, places, count, tiles, held, sems)
     for j in range(2):
         part = jnp.zeros((TILE, KW), F32)
         for k in range(4):
-            slot, live = find(places, count[0, 0], me ^ k, j)
+            copies[k, j].wait()
             product = lax.dot_general(
-                tiles[slot], images[k][...], (((0,), (0,)), ((), ())), preferred_element_type=F32
+                held[order.index((k, j))], images[k][...], (((0,), (0,)), ((), ())), preferred_element_type=F32
             )
-            part = part + jnp.where(live > 0, product, 0.0)
+            part = part + jnp.where(lives[k, j] > 0, product, 0.0)
         for y in range(2):
             for z in range(4):
                 for x in range(4):
@@ -98,8 +116,9 @@
 
 def backward(places, count, tiles, images):
     return call(
-        backward_body, [((16, 64, KW), F32)], [SMEM, SMEM] + [VMEM] * 5, (places, count, tiles, *images),
-        flops=16 * TILE * TILE * KW, moved=8 << 20,
+        backward_body, [((16, 64, KW), F32)], [SMEM, SMEM, HBM] + [VMEM] * 4, (places, count, tiles, *images),
+        scratch=[pltpu.VMEM((8, TILE, TILE), BF16), pltpu.SemaphoreType.DMA((8,))],
+        limit=20, flops=16 * TILE * TILE * KW, moved=8 << 20,
     )[0]
 
 
@@ -228,22 +247,26 @@
 
 
 def local(tile_values, tile_coords, tile_counts, sketch):
-    tiles, places = tile_values[0, 0], tile_coords[0, 0]
-    partial = [forward(q, places, tile_counts, tiles, sketch) for q in range(PARTS)]
+    tiles = pltpu.with_memory_space_constraint(tile_values[0, 0], pltpu.HBM)
+    strips = pltpu.with_memory_space_constraint(sketch, pltpu.HBM)
+    places = tile_coords[0, 0]
+    partial = [forward(q, places, tile_counts, tiles, strips) for q in range(PARTS)]
     paired = [(p[0] + swap(p[1], 1), p[2] + swap(p[3], 1)) for p in partial]
-    summed, image = [], None
-    for own, other in paired:
-        if image is not None:
-            other, image = lax.optimization_barrier((other, image))
-        image = (own + swap(other, 2)).astype(BF16)
+    sketch_rows = lax.dynamic_slice_in_dim(sketch, lax.axis_index("row") * 16, 16, 0).astype(F32)
+    images, others = [], [other for _, other in paired]
+    for q in range(PARTS):
+        image = (paired[q][0] + swap(others[q], 2)).astype(BF16)
+        image, *others = lax.optimization_barrier((image, *others))
         across = swap(image, 2)
-        four = (image, swap(image, 1), across, swap(across, 1))
-        summed.append(jnp.sum(trade(backward(places, tile_counts, tiles, four), PLANES), axis=0))
+        images.append((image, swap(image, 1), across, swap(across, 1)))
+    summed = []
+    for four in images:
+        part = backward(places, tile_counts, tiles, four)
+        part, sketch_rows, *summed = lax.optimization_barrier((part, sketch_rows, *summed))
+        summed.append(jnp.sum(trade(part, PLANES), axis=0))
     summed = jnp.concatenate(summed, axis=1)
     summed = jnp.sum(trade(summed.reshape(4, 16, K), COLUMNS), axis=0)
-    own_count = summed.shape[0]
-    offset = lax.axis_index("row") * own_count
-    shifted = summed + shift_weight * lax.dynamic_slice_in_dim(sketch, offset, own_count, 0).astype(F32)
+    shifted = summed + shift_weight * sketch_rows
     own, other = gram_parts(shifted, sketch.shape[0] * 4)
     basis, triangle = call(
         factor_body, [((16, K), F32), ((K, K), F32)], [VMEM] * 3, (own, other, shifted),

time: 293 us -> 293 us (level)
  blocking collectives: 35 us -> 83.5 us
  waiting for transfers between devices: 108 us -> 68.3 us
  starting transfers between devices: 50.5 us -> 36.6 us
  Pallas kernels: 82.4 us -> 91.8 us
  local copies, waits for them, and re-layouts: 6.94 us -> 0.98 us
    all_to_all x2 -> x4, blocking collectives: 35 us -> 83.5 us  [trade(): lax.all_to_all(value, 'row', 0, 0, tiled=True, axis_index_groups=groups)]
    all_to_all x3 -> x1, waiting for transfers between devices: 38.4 us -> 0.01 us  [trade(): lax.all_to_all(value, 'row', 0, 0, tiled=True, axis_index_groups=groups)]
    all_to_all x3 -> x1, starting transfers between devices: 19.6 us -> 5.87 us  [trade(): lax.all_to_all(value, 'row', 0, 0, tiled=True, axis_index_groups=groups)]
    pallas_call x6, Pallas kernels: 82.4 us -> 91.8 us  [call(): pl.pallas_call(body, out_shape=tuple((jax.ShapeDtypeStruct(shape, dtype)...]
    unnamed x6 -> x0, local copies, waits for them, and re-layouts: 5.96 us -> none
  transfers between devices with their start and end apart: 20 -> 18, of which waited for: 14 -> 12; matrix products, arithmetic and copies ran while one was open for 2% -> 1% of each run, Pallas kernels for 4% -> 6%
where the time goes in v1:
time: 293 us; the launch traced here: 291 us
  Pallas kernels  91.8 us (31%)
  blocking collectives  83.5 us (28%)
  waiting for transfers between devices  68.3 us (23%)
  starting transfers between devices  36.6 us (12%)
  other arithmetic  8.04 us (3%)
    pallas_call x6, Pallas kernels, call(): pl.pallas_call(body, out_shape=tuple((jax.ShapeDtypeStruct(shape, dtype)...  91.8 us
    all_to_all x4, blocking collectives, trade(): lax.all_to_all(value, 'row', 0, 0, tiled=True, axis_index_groups=groups)  83.5 us
    ppermute x15, waiting for transfers between devices, swap(): return lax.ppermute(value, 'col', [(c, c ^ bit) for c in range(4)])  63.4 us
    ppermute x15, starting transfers between devices, swap(): return lax.ppermute(value, 'col', [(c, c ^ bit) for c in range(4)])  24 us
    ppermute x2, starting transfers between devices, swap_level(): return lax.ppermute(value, 'row', [(r, r ^ bit * 4) for r in range(64)])  6.74 us
    all_to_all x1, starting transfers between devices, trade(): lax.all_to_all(value, 'row', 0, 0, tiled=True, axis_index_groups=groups)  5.87 us
  transfers between devices with their start and end apart: 18, of which 12 were waited for; matrix products, arithmetic and copies ran while one was open for 1% of the time, Pallas kernels for 6%

profile of v1, /device:TPU:1, one launch (start us, length us, event | category | flops | bytes accessed | tf_op | source)
XLA Modules:
  0.0 290.7 jit_solution(5955450205347691587)
XLA Ops:
  0.6 0.8 copy.12.places
  2.0 5.6 %shard_map.60 = (f32[512,512]{1,0:T(8,128)S(1)}, f32[512,512]{1,0:T(8,128)S(1)}, f32[512,512]{1,0:T(8,128)S(1)}, f32[512,512]{1,0:T(8,128)S(1)}) custom-call(s32[8,2]{1,0:T(8,128)S(1)} %copy.12.places, s32[1,1]{1,0:T(1,128)S(6)} %copy.14.count, bf16[8,512,512]{2,1,0:T(8,128)(2,1)} %bitcast.4, bf16[1024,1024]{1,0:T(8,128)(2,1)} %sketch.3), custom_call_target="tpu_custom_call" | custom-call | flops 2147483648 | bytes 9437184 | tf_op jit(solution)/shard_map/pallas_call | solution.py:27
  7.6 3.3 %collective-permute-start.2 = (f32[512,512]{1,0:T(8,128)S(1)}, f32[512,512]{1,0:T(8,128)S(1)}, u32[]{:S(2)}, u32[]{:S(2)}) collective-permute-start(f32[512,512]{1,0:T(8,128)S(1)} %get-tuple-element.27), channel_id=1, source_target_pairs={{0,1},{1,0},{2,3},{3,2},{4,5},{5,4},{6,7},{7,6},{8,9},{9,8},{10,11... | collective-permute-start | bytes 3145736 | tf_op jit(solution)/shard_map/ppermute | solution.py:47
  11.0 6.1 %shard_map.59 = (f32[512,512]{1,0:T(8,128)S(1)}, f32[512,512]{1,0:T(8,128)}, f32[512,512]{1,0:T(8,128)S(1)}, f32[512,512]{1,0:T(8,128)S(1)}) custom-call(s32[8,2]{1,0:T(8,128)S(1)} %copy.12.places, s32[1,1]{1,0:T(1,128)S(6)} %copy.14.count, bf16[8,512,512]{2,1,0:T(8,128)(2,1)} %bitcast.5, bf16[1024,1024]{1,0:T(8,128)(2,1)} %sketch.3), custom_call_target="tpu_custom_call" | custom-call | flops 2147483648 | bytes 9437184 | tf_op jit(solution)/shard_map/pallas_call | solution.py:27
  17.1 0.5 collective-permute-start.4
  17.7 0.2 add.38
  17.9 0.2 collective-permute-start.3
  18.1 1.8 collective-permute-done.4
  19.9 1.2 add.40
  21.1 21.5 %collective-permute-done.3 = f32[512,512]{1,0:T(8,128)S(1)} collective-permute-done((f32[512,512]{1,0:T(8,128)S(1)}, f32[512,512]{1,0:T(8,128)S(1)}, u32[]{:S(2)}, u32[]{:S(2)}) %collective-permute-start.3) | collective-permute-done | bytes 1048608 | tf_op jit(solution)/shard_map/ppermute | solution.py:47
  42.7 0.4 add_convert_fusion.1.i0
  43.1 0.3 collective-permute-start.10
  43.4 1.1 collective-permute-start.9
  44.5 11.3 %collective-permute-done.10.i2 = bf16[512,512]{1,0:T(8,128)(2,1)S(1)} collective-permute-done((bf16[512,512]{1,0:T(8,128)(2,1)S(1)}, bf16[512,512]{1,0:T(8,128)(2,1)S(1)}, u32[]{:S(2)}, u32[]{:S(2)}) %collective-permute-start.10) | collective-permute-done | bytes 524320 | tf_op jit(solution)/shard_map/ppermute | solution.py:47
  55.8 1.7 collective-permute-start.11
  57.5 0.2 collective-permute-start.5
  57.7 0.8 dynamic-slice_convert_fusion
  58.5 1.3 collective-permute-done.11.i3
  59.8 6.8 %shard_map.62 = f32[16,64,512]{2,1,0:T(8,128)} custom-call(s32[8,2]{1,0:T(8,128)S(1)} %copy.12.places, s32[1,1]{1,0:T(1,128)S(6)} %copy.14.count, bf16[8,512,512]{2,1,0:T(8,128)(2,1)} %bitcast.6, bf16[512,512]{1,0:T(8,128)(2,1)S(1)} %add_convert_fusion.1.i0, bf16[512,512]{1,0:T(8,128)(2,1)S(1)} %collective-permute-done.9.i1, ...), custom_call_target="tpu_custom_call" | custom-call | flops 2147483648 | bytes 8388608 | tf_op jit(solution)/shard_map/pallas_call | solution.py:27
  66.6 5.9 %all-to-all-start = ((f32[16,64,512]{2,1,0:T(8,128)}), f32[16,64,512]{2,1,0:T(8,128)}, u32[]{:S(2)}, u32[]{:S(2)}) async-start(f32[16,64,512]{2,1,0:T(8,128)} %shard_map.62), calls=%async_computation | async-start | bytes 4194304 | tf_op jit(solution)/shard_map/all_to_all | solution.py:43
  72.4 9.6 %collective-permute-done.5 = f32[512,512]{1,0:T(8,128)} collective-permute-done((f32[512,512]{1,0:T(8,128)}, f32[512,512]{1,0:T(8,128)}, u32[]{:S(2)}, u32[]{:S(2)}) %collective-permute-start.5) | collective-permute-done | bytes 1048608 | tf_op jit(solution)/shard_map/ppermute | solution.py:47
  82.0 1.9 add_convert_fusion.i0
  83.9 0.3 collective-permute-start.7
  84.2 1.6 collective-permute-start.6
  85.8 10.3 %collective-permute-done.7.i2 = bf16[512,512]{1,0:T(8,128)(2,1)S(1)} collective-permute-done((bf16[512,512]{1,0:T(8,128)(2,1)S(1)}, bf16[512,512]{1,0:T(8,128)(2,1)S(1)}, u32[]{:S(2)}, u32[]{:S(2)}) %collective-permute-start.7) | collective-permute-done | bytes 524320 | tf_op jit(solution)/shard_map/ppermute | solution.py:47
  96.2 2.2 collective-permute-start.8
  98.3 1.5 collective-permute-done.8.i3
  99.9 5.5 %shard_map.61 = f32[16,64,512]{2,1,0:T(8,128)S(1)} custom-call(s32[8,2]{1,0:T(8,128)S(1)} %copy.12.places, s32[1,1]{1,0:T(1,128)S(6)} %copy.14.count, bf16[8,512,512]{2,1,0:T(8,128)(2,1)} %bitcast.7, bf16[512,512]{1,0:T(8,128)(2,1)S(1)} %add_convert_fusion.i0, bf16[512,512]{1,0:T(8,128)(2,1)S(1)} %collective-permute-done.6.i1, ...), custom_call_target="tpu_custom_call" | custom-call | flops 2147483648 | bytes 8388608 | tf_op jit(solution)/shard_map/pallas_call | solution.py:27
  105.4 1.8 reduce_sum.27
  107.1 33.2 %all_to_all.25 = f32[16,64,512]{2,1,0:T(8,128)} all-to-all(f32[16,64,512]{2,1,0:T(8,128)S(1)} %shard_map.61), channel_id=1, replica_groups={{0,4,8,12,64,68,72,76,128,132,136,140,192,196,200,204},{16,20,24,28,80,..., dimensions={0} | all-to-all | bytes 4194304 | tf_op jit(solution)/shard_map/all_to_all | solution.py:43
  140.4 1.8 reduce_sum.28
  142.2 15.8 %all_to_all.26 = f32[4,16,1024]{2,1,0:T(8,128)S(1)} all-to-all(f32[4,16,1024]{2,1,0:T(8,128)S(1)} %bitcast.8), channel_id=1, replica_groups={{0,16,32,48},{4,20,36,52},{8,24,40,56},{12,28,44,60},{64,80,96,112},{68..., dimensions={0} | all-to-all | bytes 524288 | tf_op jit(solution)/shard_map/all_to_all | solution.py:43
  158.0 0.1 broadcast_in_dim.6
  158.1 16.7 %all_to_all.27.rows_in = f32[16,16,1024]{2,1,0:T(8,128)S(1)} all-to-all(f32[16,16,1024]{2,1,0:T(8,128)S(1)} %broadcast_in_dim.6), channel_id=1, replica_groups={{0,4,8,12,64,68,72,76,128,132,136,140,192,196,200,204},{16,20,24,28,80,..., dimensions={0} | all-to-all | bytes 2097152 | tf_op jit(solution)/shard_map/all_to_all | solution.py:43
  174.8 0.7 shard_map.63
  175.4 4.9 %collective-permute-start.12 = (f32[32,640]{1,0:T(8,128)S(1)}, f32[32,640]{1,0:T(8,128)S(1)}, u32[]{:S(2)}, u32[]{:S(2)}) collective-permute-start(f32[32,640]{1,0:T(8,128)S(1)} %get-tuple-element.39), channel_id=1, source_target_pairs={{0,1},{1,0},{2,3},{3,2},{4,5},{5,4},{6,7},{7,6},{8,9},{9,8},{10,11... | collective-permute-start | bytes 245768 | tf_op jit(solution)/shard_map/ppermute | solution.py:47
  180.3 0.9 collective-permute-done.12
  181.3 1.7 collective-permute-start.13
  182.9 2.4 collective-permute-done.13
  185.3 2.0 collective-permute-start.14
  187.4 2.2 collective-permute-done.14
  189.6 4.7 %collective-permute-start.15 = (f32[32,640]{1,0:T(8,128)S(1)}, f32[32,640]{1,0:T(8,128)S(1)}, u32[]{:S(2)}, u32[]{:S(2)}) collective-permute-start(f32[32,640]{1,0:T(8,128)S(1)} %add.46), channel_id=1, source_target_pairs={{0,32},{4,36},{8,40},{12,44},{16,48},{20,52},{24,56},{28,60},{32,0... | collective-permute-start | bytes 245768 | tf_op jit(solution)/shard_map/ppermute | solution.py:51
  194.3 2.7 collective-permute-done.15
  197.0 0.1 broadcast_in_dim.7
  197.2 17.8 %all_to_all.28.own = f32[16,32,640]{2,1,0:T(8,128)S(1)} all-to-all(f32[16,32,640]{2,1,0:T(8,128)S(1)} %broadcast_in_dim.7), channel_id=1, replica_groups={{0,4,8,12,64,68,72,76,128,132,136,140,192,196,200,204},{16,20,24,28,80,..., dimensions={0} | all-to-all | bytes 2621440 | tf_op jit(solution)/shard_map/all_to_all | solution.py:43
  215.0 5.8 %collective-permute-start.16 = (f32[16,32,640]{2,1,0:T(8,128)S(1)}, f32[16,32,640]{2,1,0:T(8,128)S(1)}, u32[]{:S(2)}, u32[]{:S(2)}) collective-permute-start(f32[16,32,640]{2,1,0:T(8,128)S(1)} %all_to_all.28.own), channel_id=1, source_target_pairs={{0,1},{1,0},{2,3},{3,2},{4,5},{5,4},{6,7},{7,6},{8,9},{9,8},{10,11... | collective-permute-start | bytes 3932168 | tf_op jit(solution)/shard_map/ppermute | solution.py:47
  220.8 2.7 collective-permute-done.16.other
  223.5 67.2 %shard_map.64 = (f32[16,1024]{1,0:T(8,128)}, f32[1024,1024]{1,0:T(8,128)}) custom-call(f32[16,32,640]{2,1,0:T(8,128)S(1)} %all_to_all.28.own, f32[16,32,640]{2,1,0:T(8,128)S(1)} %collective-permute-done.16.other, f32[16,1024]{1,0:T(8,128)S(1)} %multiply_add_fusion.shifted), custom_call_target="tpu_custom_call" | custom-call | flops 4294967296 | bytes 8388608 | tf_op jit(solution)/shard_map/pallas_call | solution.py:27
  (15 shorter events, 0.2 us)
Async XLA Ops:
  7.6 10.1 %collective-permute-start.2 = (f32[512,512]{1,0:T(8,128)S(1)}, f32[512,512]{1,0:T(8,128)S(1)}, u32[]{:S(2)}, u32[]{:S(2)}) collective-permute-start(f32[512,512]{1,0:T(8,128)S(1)} %get-tuple-element.27), channel_id=1, source_target_pairs={{0,1},{1,0},{2,3},{3,2},{4,5},{5,4},{6,7},{7,6},{8,9},{9,8},{10,11... | collective-permute-start | bytes 3145736 | tf_op jit(solution)/shard_map/ppermute | solution.py:47
  10.9 10.2 %collective-permute-start.1 = (f32[512,512]{1,0:T(8,128)S(1)}, f32[512,512]{1,0:T(8,128)S(1)}, u32[]{:S(2)}, u32[]{:S(2)}) collective-permute-start(f32[512,512]{1,0:T(8,128)S(1)} %get-tuple-element.25), channel_id=1, source_target_pairs={{0,1},{1,0},{2,3},{3,2},{4,5},{5,4},{6,7},{7,6},{8,9},{9,8},{10,11... | collective-permute-start | bytes 3145736 | tf_op jit(solution)/shard_map/ppermute | solution.py:47
  17.1 2.8 collective-permute-start.4
  17.9 24.8 %collective-permute-start.3 = (f32[512,512]{1,0:T(8,128)S(1)}, f32[512,512]{1,0:T(8,128)S(1)}, u32[]{:S(2)}, u32[]{:S(2)}) collective-permute-start(f32[512,512]{1,0:T(8,128)S(1)} %add.38), channel_id=1, source_target_pairs={{0,2},{1,3},{2,0},{3,1},{4,6},{5,7},{6,4},{7,5},{8,10},{9,11},{10,... | collective-permute-start | bytes 3145736 | tf_op jit(solution)/shard_map/ppermute | solution.py:47
  43.1 12.7 %collective-permute-start.10 = (bf16[512,512]{1,0:T(8,128)(2,1)S(1)}, bf16[512,512]{1,0:T(8,128)(2,1)S(1)}, u32[]{:S(2)}, u32[]{:S(2)}) collective-permute-start(bf16[512,512]{1,0:T(8,128)(2,1)S(1)} %add_convert_fusion.1.i0), channel_id=1, source_target_pairs={{0,2},{1,3},{2,0},{3,1},{4,6},{5,7},{6,4},{7,5},{8,10},{9,11},{10,... | collective-permute-start | bytes 1572872 | tf_op jit(solution)/shard_map/ppermute | solution.py:47
  43.4 15.1 %collective-permute-start.9 = (bf16[512,512]{1,0:T(8,128)(2,1)S(1)}, bf16[512,512]{1,0:T(8,128)(2,1)S(1)}, u32[]{:S(2)}, u32[]{:S(2)}) collective-permute-start(bf16[512,512]{1,0:T(8,128)(2,1)S(1)} %add_convert_fusion.1.i0), channel_id=1, source_target_pairs={{0,1},{1,0},{2,3},{3,2},{4,5},{5,4},{6,7},{7,6},{8,9},{9,8},{10,11... | collective-permute-start | bytes 1572872 | tf_op jit(solution)/shard_map/ppermute | solution.py:47
  55.8 4.0 %collective-permute-start.11 = (bf16[512,512]{1,0:T(8,128)(2,1)S(1)}, bf16[512,512]{1,0:T(8,128)(2,1)S(1)}, u32[]{:S(2)}, u32[]{:S(2)}) collective-permute-start(bf16[512,512]{1,0:T(8,128)(2,1)S(1)} %collective-permute-done.10.i2), channel_id=1, source_target_pairs={{0,1},{1,0},{2,3},{3,2},{4,5},{5,4},{6,7},{7,6},{8,9},{9,8},{10,11... | collective-permute-start | bytes 1572872 | tf_op jit(solution)/shard_map/ppermute | solution.py:47
  57.5 14.9 %collective-permute-start = (f32[512,512]{1,0:T(8,128)}, f32[512,512]{1,0:T(8,128)}, u32[]{:S(2)}, u32[]{:S(2)}) collective-permute-start(f32[512,512]{1,0:T(8,128)} %get-tuple-element.23), channel_id=1, source_target_pairs={{0,1},{1,0},{2,3},{3,2},{4,5},{5,4},{6,7},{7,6},{8,9},{9,8},{10,11... | collective-permute-start | bytes 3145736 | tf_op jit(solution)/shard_map/ppermute | solution.py:47
  57.5 24.5 %collective-permute-start.5 = (f32[512,512]{1,0:T(8,128)}, f32[512,512]{1,0:T(8,128)}, u32[]{:S(2)}, u32[]{:S(2)}) collective-permute-start(f32[512,512]{1,0:T(8,128)} %add.40), channel_id=1, source_target_pairs={{0,2},{1,3},{2,0},{3,1},{4,6},{5,7},{6,4},{7,5},{8,10},{9,11},{10,... | collective-permute-start | bytes 3145736 | tf_op jit(solution)/shard_map/ppermute | solution.py:47
  66.6 38.8 %all-to-all-start = ((f32[16,64,512]{2,1,0:T(8,128)}), f32[16,64,512]{2,1,0:T(8,128)}, u32[]{:S(2)}, u32[]{:S(2)}) async-start(f32[16,64,512]{2,1,0:T(8,128)} %shard_map.62), calls=%async_computation | async-start | bytes 4194304 | tf_op jit(solution)/shard_map/all_to_all | solution.py:43
  83.9 12.2 %collective-permute-start.7 = (bf16[512,512]{1,0:T(8,128)(2,1)S(1)}, bf16[512,512]{1,0:T(8,128)(2,1)S(1)}, u32[]{:S(2)}, u32[]{:S(2)}) collective-permute-start(bf16[512,512]{1,0:T(8,128)(2,1)S(1)} %add_convert_fusion.i0), channel_id=1, source_target_pairs={{0,2},{1,3},{2,0},{3,1},{4,6},{5,7},{6,4},{7,5},{8,10},{9,11},{10,... | collective-permute-start | bytes 1572872 | tf_op jit(solution)/shard_map/ppermute | solution.py:47
  84.2 14.1 %collective-permute-start.6 = (bf16[512,512]{1,0:T(8,128)(2,1)S(1)}, bf16[512,512]{1,0:T(8,128)(2,1)S(1)}, u32[]{:S(2)}, u32[]{:S(2)}) collective-permute-start(bf16[512,512]{1,0:T(8,128)(2,1)S(1)} %add_convert_fusion.i0), channel_id=1, source_target_pairs={{0,1},{1,0},{2,3},{3,2},{4,5},{5,4},{6,7},{7,6},{8,9},{9,8},{10,11... | collective-permute-start | bytes 1572872 | tf_op jit(solution)/shard_map/ppermute | solution.py:47
  96.2 3.7 %collective-permute-start.8 = (bf16[512,512]{1,0:T(8,128)(2,1)S(1)}, bf16[512,512]{1,0:T(8,128)(2,1)S(1)}, u32[]{:S(2)}, u32[]{:S(2)}) collective-permute-start(bf16[512,512]{1,0:T(8,128)(2,1)S(1)} %collective-permute-done.7.i2), channel_id=1, source_target_pairs={{0,1},{1,0},{2,3},{3,2},{4,5},{5,4},{6,7},{7,6},{8,9},{9,8},{10,11... | collective-permute-start | bytes 1572872 | tf_op jit(solution)/shard_map/ppermute | solution.py:47
  175.4 5.8 %collective-permute-start.12 = (f32[32,640]{1,0:T(8,128)S(1)}, f32[32,640]{1,0:T(8,128)S(1)}, u32[]{:S(2)}, u32[]{:S(2)}) collective-permute-start(f32[32,640]{1,0:T(8,128)S(1)} %get-tuple-element.39), channel_id=1, source_target_pairs={{0,1},{1,0},{2,3},{3,2},{4,5},{5,4},{6,7},{7,6},{8,9},{9,8},{10,11... | collective-permute-start | bytes 245768 | tf_op jit(solution)/shard_map/ppermute | solution.py:47
  181.3 4.1 %collective-permute-start.13 = (f32[32,640]{1,0:T(8,128)S(1)}, f32[32,640]{1,0:T(8,128)S(1)}, u32[]{:S(2)}, u32[]{:S(2)}) collective-permute-start(f32[32,640]{1,0:T(8,128)S(1)} %add.44), channel_id=1, source_target_pairs={{0,2},{1,3},{2,0},{3,1},{4,6},{5,7},{6,4},{7,5},{8,10},{9,11},{10,... | collective-permute-start | bytes 245768 | tf_op jit(solution)/shard_map/ppermute | solution.py:47
  185.3 4.3 %collective-permute-start.14 = (f32[32,640]{1,0:T(8,128)S(1)}, f32[32,640]{1,0:T(8,128)S(1)}, u32[]{:S(2)}, u32[]{:S(2)}) collective-permute-start(f32[32,640]{1,0:T(8,128)S(1)} %add.45), channel_id=1, source_target_pairs={{0,16},{4,20},{8,24},{12,28},{16,0},{20,4},{24,8},{28,12},{32,48},... | collective-permute-start | bytes 245768 | tf_op jit(solution)/shard_map/ppermute | solution.py:51
  189.6 7.4 %collective-permute-start.15 = (f32[32,640]{1,0:T(8,128)S(1)}, f32[32,640]{1,0:T(8,128)S(1)}, u32[]{:S(2)}, u32[]{:S(2)}) collective-permute-start(f32[32,640]{1,0:T(8,128)S(1)} %add.46), channel_id=1, source_target_pairs={{0,32},{4,36},{8,40},{12,44},{16,48},{20,52},{24,56},{28,60},{32,0... | collective-permute-start | bytes 245768 | tf_op jit(solution)/shard_map/ppermute | solution.py:51
  215.0 8.5 %collective-permute-start.16 = (f32[16,32,640]{2,1,0:T(8,128)S(1)}, f32[16,32,640]{2,1,0:T(8,128)S(1)}, u32[]{:S(2)}, u32[]{:S(2)}) collective-permute-start(f32[16,32,640]{2,1,0:T(8,128)S(1)} %all_to_all.28.own), channel_id=1, source_target_pairs={{0,1},{1,0},{2,3},{3,2},{4,5},{5,4},{6,7},{7,6},{8,9},{9,8},{10,11... | collective-permute-start | bytes 3932168 | tf_op jit(solution)/shard_map/ppermute | solution.py:47

commit v2 on v1

--- a/solution.py
+++ b/solution.py
@@ -12,9 +12,8 @@
 HI = lax.Precision.HIGHEST
 TILE = 512
 K = 1024
-PARTS = 2
+PARTS = 4
 KW = K // PARTS
-KH = KW // 2
 NB = 128
 shift_weight = 0.5
 
@@ -69,30 +68,41 @@
     return copies, lives
 
 
-def forward_body(first, places, count, tiles, sketch, o0, o1, o2, o3, held, strip, sems):
-    outs = (o0, o1, o2, o3)
+def forward_body(parts, places, count, tiles, sketch, *rest):
+    outs, held, strip, sems = rest[:-3], rest[-3], rest[-2], rest[-1]
     order = [(k, j) for k in (1, 3, 0, 2) for j in range(2)]
-    load = pltpu.make_async_copy(sketch.at[:, pl.ds(first, KW)], strip, sems.at[8])
+    width = len(parts) * KW
+    load = pltpu.make_async_copy(sketch.at[:, pl.ds(parts[0] * KW, width)], strip, sems.at[8])
     load.start()
     copies, lives = start_tiles(order, places, count, tiles, held, sems)
     load.wait()
     for k in (1, 3, 0, 2):
-        total = jnp.zeros((TILE, KW), F32)
+        total = jnp.zeros((TILE, width), F32)
         for j in range(2):
             copies[k, j].wait()
             tile = held[order.index((k, j))]
             product = jnp.dot(tile, strip[j * TILE:(j + 1) * TILE, :], preferred_element_type=F32)
             total = total + jnp.where(lives[k, j] > 0, product, 0.0)
-        outs[k][...] = total
-
-
-def forward(q, places, count, tiles, sketch):
-    return call(
-        functools.partial(forward_body, q * KW), [((TILE, KW), F32)] * 4, [SMEM, SMEM, HBM, HBM],
+        for n in range(len(parts)):
+            piece = total[:, n * KW:(n + 1) * KW]
+            if k % 2:
+                outs[3 * n + 2][k // 2] = piece
+            else:
+                outs[3 * n + k // 2][...] = piece
+
+
+def forward(parts, places, count, tiles, sketch):
+    width = len(parts) * KW
+    outs = call(
+        functools.partial(forward_body, parts),
+        [((TILE, KW), F32), ((TILE, KW), F32), ((2, TILE, KW), F32)] * len(parts), [SMEM, SMEM, HBM, HBM],
         (places, count, tiles, sketch),
-        scratch=[pltpu.VMEM((8, TILE, TILE), BF16), pltpu.VMEM((2 * TILE, KW), BF16), pltpu.SemaphoreType.DMA((9,))],
-        limit=20, flops=16 * TILE * TILE * KW, moved=9 << 20,
-    )
+        scratch=[
+            pltpu.VMEM((8, TILE, TILE), BF16), pltpu.VMEM((2 * TILE, width), BF16), pltpu.SemaphoreType.DMA((9,)),
+        ],
+        limit=20,
+    )
+    return [outs[3 * n:3 * n + 3] for n in range(len(parts))]
 
 
 def backward_body(places, count, tiles, i0, i1, i2, i3, out, held, sems):
@@ -118,35 +128,49 @@
     return call(
         backward_body, [((16, 64, KW), F32)], [SMEM, SMEM, HBM] + [VMEM] * 4, (places, count, tiles, *images),
         scratch=[pltpu.VMEM((8, TILE, TILE), BF16), pltpu.SemaphoreType.DMA((8,))],
-        limit=20, flops=16 * TILE * TILE * KW, moved=8 << 20,
+        limit=20,
     )[0]
 
 
+def join_body(s0, s1, s2, last, out):
+    for n, held in enumerate((s0, s1, s2)):
+        for z in range(4):
+            out[z, :, n * KW:(n + 1) * KW] = held[z * 16:(z + 1) * 16, :]
+    for z in range(4):
+        total = last[0, z * 16:(z + 1) * 16, :]
+        for p in range(1, 16):
+            total = total + last[p, z * 16:(z + 1) * 16, :]
+        out[z, :, 3 * KW:] = total
+
+
 WIDE = 5 * NB
 
 
-def strip_body(scale, rows_in, keep, give, rows, strip):
+def finish_body(got, sketch_rows, shifted, spread):
+    total = (got[0] + got[1]) + (got[2] + got[3]) + shift_weight * sketch_rows[...].astype(F32)
+    shifted[...] = total
     for p in range(16):
-        rows[p * 16:(p + 1) * 16, :K] = rows_in[p]
-        rows[p * 16:(p + 1) * 16, K:] = rows_in[p, :, :WIDE]
-    row = lax.axis_index("row")
-    x = lax.rem(row, 4)
-    start = pl.multiple_of(((row // 16) * 2 + x // 2) * NB, NB)
+        for d in range(5):
+            block = (p // 2 + d) % 8
+            spread[p, :, d * NB:(d + 1) * NB] = total[:, block * NB:(block + 1) * NB]
+
+
+def strip_body(scale, rows_in, keep, give, strip):
+    rows = jnp.concatenate([rows_in[p] for p in range(16)], axis=0)
     strip[...] = scale * lax.dot_general(
-        rows[:, pl.ds(start, NB)], rows[:, pl.ds(start, WIDE)], (((0,), (0,)), ((), ())),
-        precision=HI, preferred_element_type=F32,
+        rows[:, :NB], rows, (((0,), (0,)), ((), ())), precision=HI, preferred_element_type=F32
     )
     core = lax.rem(lax.axis_index("col"), 2)
-    half = lax.rem(x, 2) * 64
+    half = lax.rem(lax.axis_index("row"), 2) * 64
     keep[...] = strip[pl.ds(pl.multiple_of(half + core * 32, 32), 32), :]
     give[...] = strip[pl.ds(pl.multiple_of(half + (1 - core) * 32, 32), 32), :]
 
 
-def gram_parts(shifted, total_columns):
-    rows = trade(jnp.broadcast_to(shifted[None], (16, *shifted.shape)), PLANES)
+def gram_parts(spread, total_columns):
+    rows = trade(spread, PLANES)
     keep, give = call(
         functools.partial(strip_body, 1.0 / total_columns), [((32, WIDE), F32)] * 2, [VMEM], (rows,),
-        scratch=[pltpu.VMEM((256, K + WIDE), F32), pltpu.VMEM((NB, WIDE), F32)],
+        scratch=[pltpu.VMEM((NB, WIDE), F32)], limit=16,
         flops=12 * 256 * NB * WIDE, moved=2 << 20,
     )
     total = keep + swap(give, 1)
@@ -246,28 +270,51 @@
     lax.fori_loop(0, K // NB, panel, 0)
 
 
+def after(value, *others):
+    return lax.optimization_barrier((value, *others))[0]
+
+
 def local(tile_values, tile_coords, tile_counts, sketch):
     tiles = pltpu.with_memory_space_constraint(tile_values[0, 0], pltpu.HBM)
     strips = pltpu.with_memory_space_constraint(sketch, pltpu.HBM)
     places = tile_coords[0, 0]
-    partial = [forward(q, places, tile_counts, tiles, strips) for q in range(PARTS)]
-    paired = [(p[0] + swap(p[1], 1), p[2] + swap(p[3], 1)) for p in partial]
-    sketch_rows = lax.dynamic_slice_in_dim(sketch, lax.axis_index("row") * 16, 16, 0).astype(F32)
-    images, others = [], [other for _, other in paired]
+    sketch_rows = lax.dynamic_slice_in_dim(sketch, lax.axis_index("row") * 16, 16, 0)
+
+    owns, others = [], []
+
+    def pair(part):
+        got = swap(part[2], 1)
+        owns.append(part[0] + got[0])
+        others.append(part[1] + got[1])
+
+    for part in forward(list(range(PARTS)), places, tile_counts, tiles, strips):
+        pair(part)
+    images, crossed = [], []
     for q in range(PARTS):
-        image = (paired[q][0] + swap(others[q], 2)).astype(BF16)
-        image, *others = lax.optimization_barrier((image, *others))
-        across = swap(image, 2)
-        images.append((image, swap(image, 1), across, swap(across, 1)))
+        got = swap(others[q] if q < 2 else after(others[q], images[q - 2]), 2)
+        if q == 0:
+            got, others[1] = lax.optimization_barrier((got, others[1]))
+        images.append((owns[q] + got).astype(BF16))
+    for q in range(PARTS):
+        crossed.append(swap(images[q], 2))
     summed = []
-    for four in images:
+    for q, image in enumerate(images):
+        across = crossed[q]
+        if q < PARTS - 1:
+            across, images[q + 1] = lax.optimization_barrier((across, images[q + 1]))
+        four = (image, swap(image, 1), across, swap(across, 1))
         part = backward(places, tile_counts, tiles, four)
-        part, sketch_rows, *summed = lax.optimization_barrier((part, sketch_rows, *summed))
-        summed.append(jnp.sum(trade(part, PLANES), axis=0))
-    summed = jnp.concatenate(summed, axis=1)
-    summed = jnp.sum(trade(summed.reshape(4, 16, K), COLUMNS), axis=0)
-    shifted = summed + shift_weight * sketch_rows
-    own, other = gram_parts(shifted, sketch.shape[0] * 4)
+        if q == PARTS - 1:
+            part, sketch_rows, *summed = lax.optimization_barrier((part, sketch_rows, *summed))
+            summed.append(trade(part, PLANES))
+        else:
+            summed.append(jnp.sum(trade(part, PLANES), axis=0))
+    joined = call(join_body, [((4, 16, K), F32)], [VMEM] * 4, summed, limit=16, moved=2 << 20)[0]
+    shifted, spread = call(
+        finish_body, [((16, K), F32), ((16, 16, WIDE), F32)], [VMEM] * 2, (trade(joined, COLUMNS), sketch_rows),
+        limit=16, moved=1 << 20,
+    )
+    own, other = gram_parts(spread, sketch.shape[0] * 4)
     basis, triangle = call(
         factor_body, [((16, K), F32), ((K, K), F32)], [VMEM] * 3, (own, other, shifted),
         scratch=[pltpu.VMEM((K, K), F32), pltpu.VMEM((NB, NB), F32)], limit=40,

time: 293 us -> 297 us (1.014)
  starting transfers between devices: 36.6 us -> 54.4 us
  blocking collectives: 83.5 us -> 71.1 us
  waiting for transfers between devices: 68.3 us -> 58 us
  Pallas kernels: 91.8 us -> 100 us
    all_to_all x1 -> x3, starting transfers between devices: 5.87 us -> 19.5 us  [trade(): lax.all_to_all(value, 'row', 0, 0, tiled=True, axis_index_groups=groups)]
    ppermute x15 -> x23, waiting for transfers between devices: 63.4 us -> 50 us  [swap(): return lax.ppermute(value, 'col', [(c, c ^ bit) for c in range(4)])]
    all_to_all x4, blocking collectives: 83.5 us -> 71.1 us  [trade(): lax.all_to_all(value, 'row', 0, 0, tiled=True, axis_index_groups=groups)]
    pallas_call x6 -> x9, Pallas kernels: 91.8 us -> 100 us  [call(): pl.pallas_call(body, out_shape=tuple((jax.ShapeDtypeStruct(shape, dtype)...]
    ppermute x15 -> x23, starting transfers between devices: 24 us -> 30.3 us  [swap(): return lax.ppermute(value, 'col', [(c, c ^ bit) for c in range(4)])]
  transfers between devices with their start and end apart: 18 -> 28, of which waited for: 12 -> 16; matrix products, arithmetic and copies ran while one was open for 1% -> 3% of each run, Pallas kernels for 6% -> 8%
where the time goes in v2:
time: 297 us; the launch traced here: 296 us
  Pallas kernels  100 us (34%)
  blocking collectives  71.1 us (24%)
  waiting for transfers between devices  58 us (20%)
  starting transfers between devices  54.4 us (18%)
  other arithmetic  8.6 us (3%)
    pallas_call x9, Pallas kernels, call(): pl.pallas_call(body, out_shape=tuple((jax.ShapeDtypeStruct(shape, dtype)...  100 us
    all_to_all x4, blocking collectives, trade(): lax.all_to_all(value, 'row', 0, 0, tiled=True, axis_index_groups=groups)  71.1 us
    ppermute x23, waiting for transfers between devices, swap(): return lax.ppermute(value, 'col', [(c, c ^ bit) for c in range(4)])  50 us
    ppermute x23, starting transfers between devices, swap(): return lax.ppermute(value, 'col', [(c, c ^ bit) for c in range(4)])  30.3 us
    all_to_all x3, starting transfers between devices, trade(): lax.all_to_all(value, 'row', 0, 0, tiled=True, axis_index_groups=groups)  19.5 us
    ppermute x2, waiting for transfers between devices, swap_level(): return lax.ppermute(value, 'row', [(r, r ^ bit * 4) for r in range(64)])  7.86 us
  transfers between devices with their start and end apart: 28, of which 16 were waited for; matrix products, arithmetic and copies ran while one was open for 3% of the time, Pallas kernels for 8%

profile of v2, /device:TPU:1, one launch (start us, length us, event | category | flops | bytes accessed | tf_op | source)
XLA Modules:
  0.0 296.1 jit_solution(13466882580479871239)
XLA Ops:
  2.0 8.1 %shard_map.59 = (f32[512,256]{1,0:T(8,128)S(1)}, f32[512,256]{1,0:T(8,128)S(1)}, f32[2,512,256]{2,1,0:T(8,128)S(1)}, f32[512,256]{1,0:T(8,128)S(1)}, f32[512,256...) custom-call(s32[8,2]{1,0:T(8,128)S(1)} %copy.7.places, ...), custom_call_target="tpu_custom_call" | custom-call | tf_op jit(solution)/shard_map/pallas_call | solution.py:26
  10.1 3.3 %collective-permute-start.1 = (f32[2,512,256]{2,1,0:T(8,128)S(1)}, f32[2,512,256]{2,1,0:T(8,128)S(1)}, u32[]{:S(2)}, u32[]{:S(2)}) collective-permute-start(f32[2,512,256]{2,1,0:T(8,128)S(1)} %get-tuple-element.39), channel_id=1, source_target_pairs={{0,1},{1,0},{2,3},{3,2},{4,5},{5,4},{6,7},{7,6},{8,9},{9,8},{10,11... | collective-permute-start | bytes 3145736 | tf_op jit(solution)/shard_map/ppermute | solution.py:46
  13.5 2.2 collective-permute-done.1
  17.3 11.7 %collective-permute-done.2 = f32[512,256]{1,0:T(8,128)S(1)} collective-permute-done((f32[512,256]{1,0:T(8,128)S(1)}, f32[512,256]{1,0:T(8,128)S(1)}, u32[]{:S(2)}, u32[]{:S(2)}) %collective-permute-start.2) | collective-permute-done | bytes 524320 | tf_op jit(solution)/shard_map/ppermute | solution.py:46
  29.2 1.4 collective-permute-start.6
  30.6 1.5 collective-permute-start.13
  32.5 8.8 %collective-permute-done.7 = f32[512,256]{1,0:T(8,128)S(1)} collective-permute-done((f32[512,256]{1,0:T(8,128)S(1)}, f32[512,256]{1,0:T(8,128)S(1)}, u32[]{:S(2)}, u32[]{:S(2)}) %collective-permute-start.7) | collective-permute-done | bytes 524320 | tf_op jit(solution)/shard_map/ppermute | solution.py:46
  41.4 5.5 %collective-permute-done.13.i2 = bf16[512,256]{1,0:T(8,128)(2,1)S(1)} collective-permute-done((bf16[512,256]{1,0:T(8,128)(2,1)S(1)}, bf16[512,256]{1,0:T(8,128)(2,1)S(1)}, u32[]{:S(2)}, u32[]{:S(2)}) %collective-permute-start.13) | collective-permute-done | bytes 262176 | tf_op jit(solution)/shard_map/ppermute | solution.py:46
  46.9 2.1 collective-permute-start.14
  49.0 1.0 fusion.12
  50.1 6.2 %shard_map.61 = f32[16,64,256]{2,1,0:T(8,128)} custom-call(s32[8,2]{1,0:T(8,128)S(1)} %copy.7.places, s32[1,1]{1,0:T(1,128)S(6)} %copy.11.count, bf16[8,512,512]{2,1,0:T(8,128)(2,1)} %bitcast.52, bf16[512,256]{1,0:T(8,128)(2,1)S(1)} %fusion.11.i0, bf16[512,256]{1,0:T(8,128)(2,1)S(1)} %collective-permute-done.12.i1, ...), custom_call_target="tpu_custom_call" | custom-call | tf_op jit(solution)/shard_map/pallas_call | solution.py:26
  56.4 6.5 %all-to-all-start = ((f32[16,64,256]{2,1,0:T(8,128)}), f32[16,64,256]{2,1,0:T(8,128)}, u32[]{:S(2)}, u32[]{:S(2)}) async-start(f32[16,64,256]{2,1,0:T(8,128)} %shard_map.61), calls=%async_computation | async-start | bytes 2097152 | tf_op jit(solution)/shard_map/all_to_all | solution.py:42
  63.2 0.9 collective-permute-start.15
  65.0 1.3 fusion.15.i0
  66.3 4.2 %collective-permute-done.16.i2 = bf16[512,256]{1,0:T(8,128)(2,1)S(1)} collective-permute-done((bf16[512,256]{1,0:T(8,128)(2,1)S(1)}, bf16[512,256]{1,0:T(8,128)(2,1)S(1)}, u32[]{:S(2)}, u32[]{:S(2)}) %collective-permute-start.16) | collective-permute-done | bytes 262176 | tf_op jit(solution)/shard_map/ppermute | solution.py:46
  70.5 1.3 collective-permute-start.17
  71.8 1.9 fusion.3
  73.9 6.3 %shard_map.62 = f32[16,64,256]{2,1,0:T(8,128)} custom-call(s32[8,2]{1,0:T(8,128)S(1)} %copy.7.places, s32[1,1]{1,0:T(1,128)S(6)} %copy.11.count, bf16[8,512,512]{2,1,0:T(8,128)(2,1)} %bitcast.53, bf16[512,256]{1,0:T(8,128)(2,1)S(1)} %fusion.2.i0, bf16[512,256]{1,0:T(8,128)(2,1)S(1)} %collective-permute-done.15.i1, ...), custom_call_target="tpu_custom_call" | custom-call | tf_op jit(solution)/shard_map/pallas_call | solution.py:26
  80.2 6.5 %all-to-all-start.1 = ((f32[16,64,256]{2,1,0:T(8,128)}), f32[16,64,256]{2,1,0:T(8,128)S(1)}, u32[]{:S(2)}, u32[]{:S(2)}) async-start(f32[16,64,256]{2,1,0:T(8,128)} %shard_map.62), calls=%async_computation.1 | async-start | bytes 2097152 | tf_op jit(solution)/shard_map/all_to_all | solution.py:42
  86.7 1.3 collective-permute-start.5
  88.9 1.3 fusion.6.i0
  90.3 3.9 %collective-permute-done.5.i2 = bf16[512,256]{1,0:T(8,128)(2,1)S(1)} collective-permute-done((bf16[512,256]{1,0:T(8,128)(2,1)S(1)}, bf16[512,256]{1,0:T(8,128)(2,1)S(1)}, u32[]{:S(2)}, u32[]{:S(2)}) %collective-permute-start.5) | collective-permute-done | bytes 262176 | tf_op jit(solution)/shard_map/ppermute | solution.py:46
  94.1 1.4 collective-permute-start.19
  95.5 1.2 collective-permute-done.19.i3
  96.7 6.2 %shard_map.63 = f32[16,64,256]{2,1,0:T(8,128)} custom-call(s32[8,2]{1,0:T(8,128)S(1)} %copy.7.places, s32[1,1]{1,0:T(1,128)S(6)} %copy.11.count, bf16[8,512,512]{2,1,0:T(8,128)(2,1)} %bitcast.54, bf16[512,256]{1,0:T(8,128)(2,1)S(1)} %fusion.15.i0, bf16[512,256]{1,0:T(8,128)(2,1)S(1)} %collective-permute-done.18.i1, ...), custom_call_target="tpu_custom_call" | custom-call | tf_op jit(solution)/shard_map/pallas_call | solution.py:26
  103.2 6.4 %all-to-all-start.2 = ((f32[16,64,256]{2,1,0:T(8,128)}), f32[16,64,256]{2,1,0:T(8,128)}, u32[]{:S(2)}, u32[]{:S(2)}) async-start(f32[16,64,256]{2,1,0:T(8,128)} %shard_map.63), calls=%async_computation.2 | async-start | bytes 2097152 | tf_op jit(solution)/shard_map/all_to_all | solution.py:42
  109.6 1.3 collective-permute-start.10
  111.0 0.9 collective-permute-start.9
  111.9 5.1 %collective-permute-done.10.i2 = bf16[512,256]{1,0:T(8,128)(2,1)S(1)} collective-permute-done((bf16[512,256]{1,0:T(8,128)(2,1)S(1)}, bf16[512,256]{1,0:T(8,128)(2,1)S(1)}, u32[]{:S(2)}, u32[]{:S(2)}) %collective-permute-start.10) | collective-permute-done | bytes 262176 | tf_op jit(solution)/shard_map/ppermute | solution.py:46
  117.0 1.4 collective-permute-start.11
  119.6 5.3 %shard_map.60 = f32[16,64,256]{2,1,0:T(8,128)S(1)} custom-call(s32[8,2]{1,0:T(8,128)S(1)} %copy.7.places, s32[1,1]{1,0:T(1,128)S(6)} %copy.11.count, bf16[8,512,512]{2,1,0:T(8,128)(2,1)} %bitcast.55, bf16[512,256]{1,0:T(8,128)(2,1)S(1)} %fusion.6.i0, bf16[512,256]{1,0:T(8,128)(2,1)S(1)} %collective-permute-done.9.i1, ...), custom_call_target="tpu_custom_call" | custom-call | tf_op jit(solution)/shard_map/pallas_call | solution.py:26
  124.9 1.3 reduce_sum.27.s0
  126.3 1.3 reduce_sum.29.s2
  127.6 22.7 %all_to_all.35.last = f32[16,64,256]{2,1,0:T(8,128)S(1)} all-to-all(f32[16,64,256]{2,1,0:T(8,128)S(1)} %shard_map.60), channel_id=1, replica_groups={{0,4,8,12,64,68,72,76,128,132,136,140,192,196,200,204},{16,20,24,28,80,..., dimensions={0} | all-to-all | bytes 2097152 | tf_op jit(solution)/shard_map/all_to_all | solution.py:42
  150.3 16.2 %all_to_all.36.got = f32[4,16,1024]{2,1,0:T(8,128)S(1)} all-to-all(f32[4,16,1024]{2,1,0:T(8,128)S(1)} %shard_map.64), channel_id=1, replica_groups={{0,16,32,48},{4,20,36,52},{8,24,40,56},{12,28,44,60},{64,80,96,112},{68..., dimensions={0} | all-to-all | bytes 524288 | tf_op jit(solution)/shard_map/all_to_all | solution.py:42
  166.5 13.0 %all_to_all.37.rows_in = f32[16,16,640]{2,1,0:T(8,128)S(1)} all-to-all(f32[16,16,640]{2,1,0:T(8,128)S(1)} %get-tuple-element.62), channel_id=1, replica_groups={{0,4,8,12,64,68,72,76,128,132,136,140,192,196,200,204},{16,20,24,28,80,..., dimensions={0} | all-to-all | bytes 1310720 | tf_op jit(solution)/shard_map/all_to_all | solution.py:42
  180.0 5.0 %collective-permute-start.20 = (f32[32,640]{1,0:T(8,128)S(1)}, f32[32,640]{1,0:T(8,128)S(1)}, u32[]{:S(2)}, u32[]{:S(2)}) collective-permute-start(f32[32,640]{1,0:T(8,128)S(1)} %get-tuple-element.64), channel_id=1, source_target_pairs={{0,1},{1,0},{2,3},{3,2},{4,5},{5,4},{6,7},{7,6},{8,9},{9,8},{10,11... | collective-permute-start | bytes 245768 | tf_op jit(solution)/shard_map/ppermute | solution.py:46
  185.0 0.9 collective-permute-done.20
  186.0 1.1 collective-permute-start.21
  187.1 2.6 collective-permute-done.21
  189.7 1.3 collective-permute-start.22
  191.0 3.9 %collective-permute-done.22 = f32[32,640]{1,0:T(8,128)S(1)} collective-permute-done((f32[32,640]{1,0:T(8,128)S(1)}, f32[32,640]{1,0:T(8,128)S(1)}, u32[]{:S(2)}, u32[]{:S(2)}) %collective-permute-start.22) | collective-permute-done | bytes 81952 | tf_op jit(solution)/shard_map/ppermute | solution.py:50
  194.9 3.3 %collective-permute-start.23 = (f32[32,640]{1,0:T(8,128)S(1)}, f32[32,640]{1,0:T(8,128)S(1)}, u32[]{:S(2)}, u32[]{:S(2)}) collective-permute-start(f32[32,640]{1,0:T(8,128)S(1)} %add.66), channel_id=1, source_target_pairs={{0,32},{4,36},{8,40},{12,44},{16,48},{20,52},{24,56},{28,60},{32,0... | collective-permute-start | bytes 245768 | tf_op jit(solution)/shard_map/ppermute | solution.py:50
  198.2 4.0 %collective-permute-done.23 = f32[32,640]{1,0:T(8,128)S(1)} collective-permute-done((f32[32,640]{1,0:T(8,128)S(1)}, f32[32,640]{1,0:T(8,128)S(1)}, u32[]{:S(2)}, u32[]{:S(2)}) %collective-permute-start.23) | collective-permute-done | bytes 81952 | tf_op jit(solution)/shard_map/ppermute | solution.py:50
  202.3 19.3 %all_to_all.38.own = f32[16,32,640]{2,1,0:T(8,128)S(1)} all-to-all(f32[16,32,640]{2,1,0:T(8,128)S(1)} %broadcast_in_dim.4), channel_id=1, replica_groups={{0,4,8,12,64,68,72,76,128,132,136,140,192,196,200,204},{16,20,24,28,80,..., dimensions={0} | all-to-all | bytes 2621440 | tf_op jit(solution)/shard_map/all_to_all | solution.py:42
  221.6 4.6 %collective-permute-start.24 = (f32[16,32,640]{2,1,0:T(8,128)S(1)}, f32[16,32,640]{2,1,0:T(8,128)S(1)}, u32[]{:S(2)}, u32[]{:S(2)}) collective-permute-start(f32[16,32,640]{2,1,0:T(8,128)S(1)} %all_to_all.38.own), channel_id=1, source_target_pairs={{0,1},{1,0},{2,3},{3,2},{4,5},{5,4},{6,7},{7,6},{8,9},{9,8},{10,11... | collective-permute-start | bytes 3932168 | tf_op jit(solution)/shard_map/ppermute | solution.py:46
  226.2 2.7 collective-permute-done.24.other
  228.8 67.2 %shard_map.67 = (f32[16,1024]{1,0:T(8,128)}, f32[1024,1024]{1,0:T(8,128)}) custom-call(f32[16,32,640]{2,1,0:T(8,128)S(1)} %all_to_all.38.own, f32[16,32,640]{2,1,0:T(8,128)S(1)} %collective-permute-done.24.other, f32[16,1024]{1,0:T(8,128)S(1)} %get-tuple-element.65.shifted), custom_call_target="tpu_custom_call" | custom-call | flops 4294967296 | bytes 8388608 | tf_op jit(solution)/shard_map/pallas_call | solution.py:26
  (43 shorter events, 7.7 us)
Async XLA Ops:
  10.1 5.6 %collective-permute-start.1 = (f32[2,512,256]{2,1,0:T(8,128)S(1)}, f32[2,512,256]{2,1,0:T(8,128)S(1)}, u32[]{:S(2)}, u32[]{:S(2)}) collective-permute-start(f32[2,512,256]{2,1,0:T(8,128)S(1)} %get-tuple-element.39), channel_id=1, source_target_pairs={{0,1},{1,0},{2,3},{3,2},{4,5},{5,4},{6,7},{7,6},{8,9},{9,8},{10,11... | collective-permute-start | bytes 3145736 | tf_op jit(solution)/shard_map/ppermute | solution.py:46
  13.4 3.8 %collective-permute-start.3 = (f32[2,512,256]{2,1,0:T(8,128)S(1)}, f32[2,512,256]{2,1,0:T(8,128)S(1)}, u32[]{:S(2)}, u32[]{:S(2)}) collective-permute-start(f32[2,512,256]{2,1,0:T(8,128)S(1)} %get-tuple-element.42), channel_id=1, source_target_pairs={{0,1},{1,0},{2,3},{3,2},{4,5},{5,4},{6,7},{7,6},{8,9},{9,8},{10,11... | collective-permute-start | bytes 3145736 | tf_op jit(solution)/shard_map/ppermute | solution.py:46
  15.8 13.2 %collective-permute-start.2 = (f32[512,256]{1,0:T(8,128)S(1)}, f32[512,256]{1,0:T(8,128)S(1)}, u32[]{:S(2)}, u32[]{:S(2)}) collective-permute-start(f32[512,256]{1,0:T(8,128)S(1)} %fusion.8), channel_id=1, source_target_pairs={{0,2},{1,3},{2,0},{3,1},{4,6},{5,7},{6,4},{7,5},{8,10},{9,11},{10,... | collective-permute-start | bytes 1572872 | tf_op jit(solution)/shard_map/ppermute | solution.py:46
  15.9 33.1 %collective-permute-start = (f32[2,512,256]{2,1,0:T(8,128)S(1)}, f32[2,512,256]{2,1,0:T(8,128)S(1)}, u32[]{:S(2)}, u32[]{:S(2)}) collective-permute-start(f32[2,512,256]{2,1,0:T(8,128)S(1)} %get-tuple-element.36), channel_id=1, source_target_pairs={{0,1},{1,0},{2,3},{3,2},{4,5},{5,4},{6,7},{7,6},{8,9},{9,8},{10,11... | collective-permute-start | bytes 3145736 | tf_op jit(solution)/shard_map/ppermute | solution.py:46
  29.0 12.2 %collective-permute-start.7 = (f32[512,256]{1,0:T(8,128)S(1)}, f32[512,256]{1,0:T(8,128)S(1)}, u32[]{:S(2)}, u32[]{:S(2)}) collective-permute-start(f32[512,256]{1,0:T(8,128)S(1)} %fusion.7), channel_id=1, source_target_pairs={{0,2},{1,3},{2,0},{3,1},{4,6},{5,7},{6,4},{7,5},{8,10},{9,11},{10,... | collective-permute-start | bytes 1572872 | tf_op jit(solution)/shard_map/ppermute | solution.py:46
  29.2 42.6 %collective-permute-start.6 = (f32[2,512,256]{2,1,0:T(8,128)S(1)}, f32[2,512,256]{2,1,0:T(8,128)}, u32[]{:S(2)}, u32[]{:S(2)}) collective-permute-start(f32[2,512,256]{2,1,0:T(8,128)S(1)} %get-tuple-element.46), channel_id=1, source_target_pairs={{0,1},{1,0},{2,3},{3,2},{4,5},{5,4},{6,7},{7,6},{8,9},{9,8},{10,11... | collective-permute-start | bytes 3145736 | tf_op jit(solution)/shard_map/ppermute | solution.py:46
  30.6 16.2 %collective-permute-start.13 = (bf16[512,256]{1,0:T(8,128)(2,1)S(1)}, bf16[512,256]{1,0:T(8,128)(2,1)S(1)}, u32[]{:S(2)}, u32[]{:S(2)}) collective-permute-start(bf16[512,256]{1,0:T(8,128)(2,1)S(1)} %fusion.11.i0), channel_id=1, source_target_pairs={{0,2},{1,3},{2,0},{3,1},{4,6},{5,7},{6,4},{7,5},{8,10},{9,11},{10,... | collective-permute-start | bytes 786440 | tf_op jit(solution)/shard_map/ppermute | solution.py:46
  32.2 17.9 %collective-permute-start.12 = (bf16[512,256]{1,0:T(8,128)(2,1)S(1)}, bf16[512,256]{1,0:T(8,128)(2,1)S(1)}, u32[]{:S(2)}, u32[]{:S(2)}) collective-permute-start(bf16[512,256]{1,0:T(8,128)(2,1)S(1)} %fusion.11.i0), channel_id=1, source_target_pairs={{0,1},{1,0},{2,3},{3,2},{4,5},{5,4},{6,7},{7,6},{8,9},{9,8},{10,11... | collective-permute-start | bytes 786440 | tf_op jit(solution)/shard_map/ppermute | solution.py:46
  46.9 3.3 %collective-permute-start.14 = (bf16[512,256]{1,0:T(8,128)(2,1)S(1)}, bf16[512,256]{1,0:T(8,128)(2,1)S(1)}, u32[]{:S(2)}, u32[]{:S(2)}) collective-permute-start(bf16[512,256]{1,0:T(8,128)(2,1)S(1)} %collective-permute-done.13.i2), channel_id=1, source_target_pairs={{0,1},{1,0},{2,3},{3,2},{4,5},{5,4},{6,7},{7,6},{8,9},{9,8},{10,11... | collective-permute-start | bytes 786440 | tf_op jit(solution)/shard_map/ppermute | solution.py:46
  49.0 1.1 copy-start
  50.0 14.2 %collective-permute-start.4 = (f32[512,256]{1,0:T(8,128)}, f32[512,256]{1,0:T(8,128)S(1)}, u32[]{:S(2)}, u32[]{:S(2)}) collective-permute-start(f32[512,256]{1,0:T(8,128)} %fusion.12), channel_id=1, source_target_pairs={{0,2},{1,3},{2,0},{3,1},{4,6},{5,7},{6,4},{7,5},{8,10},{9,11},{10,... | collective-permute-start | bytes 1572872 | tf_op jit(solution)/shard_map/ppermute | solution.py:46
  56.4 23.8 %all-to-all-start = ((f32[16,64,256]{2,1,0:T(8,128)}), f32[16,64,256]{2,1,0:T(8,128)}, u32[]{:S(2)}, u32[]{:S(2)}) async-start(f32[16,64,256]{2,1,0:T(8,128)} %shard_map.61), calls=%async_computation | async-start | bytes 2097152 | tf_op jit(solution)/shard_map/all_to_all | solution.py:42
  63.0 7.5 %collective-permute-start.16 = (bf16[512,256]{1,0:T(8,128)(2,1)S(1)}, bf16[512,256]{1,0:T(8,128)(2,1)S(1)}, u32[]{:S(2)}, u32[]{:S(2)}) collective-permute-start(bf16[512,256]{1,0:T(8,128)(2,1)S(1)} %fusion.2.i0), channel_id=1, source_target_pairs={{0,2},{1,3},{2,0},{3,1},{4,6},{5,7},{6,4},{7,5},{8,10},{9,11},{10,... | collective-permute-start | bytes 786440 | tf_op jit(solution)/shard_map/ppermute | solution.py:46
  63.2 10.7 %collective-permute-start.15 = (bf16[512,256]{1,0:T(8,128)(2,1)S(1)}, bf16[512,256]{1,0:T(8,128)(2,1)S(1)}, u32[]{:S(2)}, u32[]{:S(2)}) collective-permute-start(bf16[512,256]{1,0:T(8,128)(2,1)S(1)} %fusion.2.i0), channel_id=1, source_target_pairs={{0,1},{1,0},{2,3},{3,2},{4,5},{5,4},{6,7},{7,6},{8,9},{9,8},{10,11... | collective-permute-start | bytes 786440 | tf_op jit(solution)/shard_map/ppermute | solution.py:46
  64.2 0.8 copy-start.1
  70.5 3.5 %collective-permute-start.17 = (bf16[512,256]{1,0:T(8,128)(2,1)S(1)}, bf16[512,256]{1,0:T(8,128)(2,1)S(1)}, u32[]{:S(2)}, u32[]{:S(2)}) collective-permute-start(bf16[512,256]{1,0:T(8,128)(2,1)S(1)} %collective-permute-done.16.i2), channel_id=1, source_target_pairs={{0,1},{1,0},{2,3},{3,2},{4,5},{5,4},{6,7},{7,6},{8,9},{9,8},{10,11... | collective-permute-start | bytes 786440 | tf_op jit(solution)/shard_map/ppermute | solution.py:46
  73.7 15.2 %collective-permute-start.8 = (f32[512,256]{1,0:T(8,128)}, f32[512,256]{1,0:T(8,128)}, u32[]{:S(2)}, u32[]{:S(2)}) collective-permute-start(f32[512,256]{1,0:T(8,128)} %fusion.3), channel_id=1, source_target_pairs={{0,2},{1,3},{2,0},{3,1},{4,6},{5,7},{6,4},{7,5},{8,10},{9,11},{10,... | collective-permute-start | bytes 1572872 | tf_op jit(solution)/shard_map/ppermute | solution.py:46
  80.2 23.0 %all-to-all-start.1 = ((f32[16,64,256]{2,1,0:T(8,128)}), f32[16,64,256]{2,1,0:T(8,128)S(1)}, u32[]{:S(2)}, u32[]{:S(2)}) async-start(f32[16,64,256]{2,1,0:T(8,128)} %shard_map.62), calls=%async_computation.1 | async-start | bytes 2097152 | tf_op jit(solution)/shard_map/all_to_all | solution.py:42
  86.7 7.4 %collective-permute-start.5 = (bf16[512,256]{1,0:T(8,128)(2,1)S(1)}, bf16[512,256]{1,0:T(8,128)(2,1)S(1)}, u32[]{:S(2)}, u32[]{:S(2)}) collective-permute-start(bf16[512,256]{1,0:T(8,128)(2,1)S(1)} %fusion.15.i0), channel_id=1, source_target_pairs={{0,2},{1,3},{2,0},{3,1},{4,6},{5,7},{6,4},{7,5},{8,10},{9,11},{10,... | collective-permute-start | bytes 786440 | tf_op jit(solution)/shard_map/ppermute | solution.py:46
  88.1 7.5 %collective-permute-start.18 = (bf16[512,256]{1,0:T(8,128)(2,1)S(1)}, bf16[512,256]{1,0:T(8,128)(2,1)S(1)}, u32[]{:S(2)}, u32[]{:S(2)}) collective-permute-start(bf16[512,256]{1,0:T(8,128)(2,1)S(1)} %fusion.15.i0), channel_id=1, source_target_pairs={{0,1},{1,0},{2,3},{3,2},{4,5},{5,4},{6,7},{7,6},{8,9},{9,8},{10,11... | collective-permute-start | bytes 786440 | tf_op jit(solution)/shard_map/ppermute | solution.py:46
  94.1 2.6 collective-permute-start.19
  103.2 23.1 %all-to-all-start.2 = ((f32[16,64,256]{2,1,0:T(8,128)}), f32[16,64,256]{2,1,0:T(8,128)}, u32[]{:S(2)}, u32[]{:S(2)}) async-start(f32[16,64,256]{2,1,0:T(8,128)} %shard_map.63), calls=%async_computation.2 | async-start | bytes 2097152 | tf_op jit(solution)/shard_map/all_to_all | solution.py:42
  109.6 7.4 %collective-permute-start.10 = (bf16[512,256]{1,0:T(8,128)(2,1)S(1)}, bf16[512,256]{1,0:T(8,128)(2,1)S(1)}, u32[]{:S(2)}, u32[]{:S(2)}) collective-permute-start(bf16[512,256]{1,0:T(8,128)(2,1)S(1)} %fusion.6.i0), channel_id=1, source_target_pairs={{0,2},{1,3},{2,0},{3,1},{4,6},{5,7},{6,4},{7,5},{8,10},{9,11},{10,... | collective-permute-start | bytes 786440 | tf_op jit(solution)/shard_map/ppermute | solution.py:46
  111.0 8.2 %collective-permute-start.9 = (bf16[512,256]{1,0:T(8,128)(2,1)S(1)}, bf16[512,256]{1,0:T(8,128)(2,1)S(1)}, u32[]{:S(2)}, u32[]{:S(2)}) collective-permute-start(bf16[512,256]{1,0:T(8,128)(2,1)S(1)} %fusion.6.i0), channel_id=1, source_target_pairs={{0,1},{1,0},{2,3},{3,2},{4,5},{5,4},{6,7},{7,6},{8,9},{9,8},{10,11... | collective-permute-start | bytes 786440 | tf_op jit(solution)/shard_map/ppermute | solution.py:46
  117.0 2.6 collective-permute-start.11
  180.0 5.9 %collective-permute-start.20 = (f32[32,640]{1,0:T(8,128)S(1)}, f32[32,640]{1,0:T(8,128)S(1)}, u32[]{:S(2)}, u32[]{:S(2)}) collective-permute-start(f32[32,640]{1,0:T(8,128)S(1)} %get-tuple-element.64), channel_id=1, source_target_pairs={{0,1},{1,0},{2,3},{3,2},{4,5},{5,4},{6,7},{7,6},{8,9},{9,8},{10,11... | collective-permute-start | bytes 245768 | tf_op jit(solution)/shard_map/ppermute | solution.py:46
  186.0 3.8 %collective-permute-start.21 = (f32[32,640]{1,0:T(8,128)S(1)}, f32[32,640]{1,0:T(8,128)S(1)}, u32[]{:S(2)}, u32[]{:S(2)}) collective-permute-start(f32[32,640]{1,0:T(8,128)S(1)} %add.64), channel_id=1, source_target_pairs={{0,2},{1,3},{2,0},{3,1},{4,6},{5,7},{6,4},{7,5},{8,10},{9,11},{10,... | collective-permute-start | bytes 245768 | tf_op jit(solution)/shard_map/ppermute | solution.py:46
  189.7 5.2 %collective-permute-start.22 = (f32[32,640]{1,0:T(8,128)S(1)}, f32[32,640]{1,0:T(8,128)S(1)}, u32[]{:S(2)}, u32[]{:S(2)}) collective-permute-start(f32[32,640]{1,0:T(8,128)S(1)} %add.65), channel_id=1, source_target_pairs={{0,16},{4,20},{8,24},{12,28},{16,0},{20,4},{24,8},{28,12},{32,48},... | collective-permute-start | bytes 245768 | tf_op jit(solution)/shard_map/ppermute | solution.py:50
  194.9 7.3 %collective-permute-start.23 = (f32[32,640]{1,0:T(8,128)S(1)}, f32[32,640]{1,0:T(8,128)S(1)}, u32[]{:S(2)}, u32[]{:S(2)}) collective-permute-start(f32[32,640]{1,0:T(8,128)S(1)} %add.66), channel_id=1, source_target_pairs={{0,32},{4,36},{8,40},{12,44},{16,48},{20,52},{24,56},{28,60},{32,0... | collective-permute-start | bytes 245768 | tf_op jit(solution)/shard_map/ppermute | solution.py:50
  221.6 7.2 %collective-permute-start.24 = (f32[16,32,640]{2,1,0:T(8,128)S(1)}, f32[16,32,640]{2,1,0:T(8,128)S(1)}, u32[]{:S(2)}, u32[]{:S(2)}) collective-permute-start(f32[16,32,640]{2,1,0:T(8,128)S(1)} %all_to_all.38.own), channel_id=1, source_target_pairs={{0,1},{1,0},{2,3},{3,2},{4,5},{5,4},{6,7},{7,6},{8,9},{9,8},{10,11... | collective-permute-start | bytes 3932168 | tf_op jit(solution)/shard_map/ppermute | solution.py:46

commit v3 on v2

--- a/solution.py
+++ b/solution.py
@@ -12,7 +12,7 @@
 HI = lax.Precision.HIGHEST
 TILE = 512
 K = 1024
-PARTS = 4
+PARTS = 2
 KW = K // PARTS
 NB = 128
 shift_weight = 0.5
@@ -59,31 +59,39 @@
     return slot, live
 
 
-def start_tiles(order, places, count, tiles, held, sems):
+def start_tiles(order, places, count, tiles, target, sems):
     copies, lives = {}, {}
     for n, (k, j) in enumerate(order):
         slot, lives[k, j] = find(places, count[0, 0], lax.axis_index("col") ^ k, j)
-        copies[k, j] = pltpu.make_async_copy(tiles.at[slot], held.at[n], sems.at[n])
+        copies[k, j] = pltpu.make_async_copy(tiles.at[slot], target(k, j), sems.at[n])
         copies[k, j].start()
     return copies, lives
 
 
-def forward_body(parts, places, count, tiles, sketch, *rest):
+def finish_tile(copy, live, target):
+    copy.wait()
+
+    @pl.when(live == 0)
+    def _():
+        target[...] = jnp.zeros((TILE, TILE), BF16)
+
+
+def forward_body(places, count, tiles, sketch, *rest):
     outs, held, strip, sems = rest[:-3], rest[-3], rest[-2], rest[-1]
     order = [(k, j) for k in (1, 3, 0, 2) for j in range(2)]
-    width = len(parts) * KW
-    load = pltpu.make_async_copy(sketch.at[:, pl.ds(parts[0] * KW, width)], strip, sems.at[8])
+
+    def target(k, j):
+        return held.at[k, :, pl.ds(j * TILE, TILE)]
+
+    load = pltpu.make_async_copy(sketch, strip, sems.at[8])
     load.start()
-    copies, lives = start_tiles(order, places, count, tiles, held, sems)
+    copies, lives = start_tiles(order, places, count, tiles, target, sems)
     load.wait()
     for k in (1, 3, 0, 2):
-        total = jnp.zeros((TILE, width), F32)
         for j in range(2):
-            copies[k, j].wait()
-            tile = held[order.index((k, j))]
-            product = jnp.dot(tile, strip[j * TILE:(j + 1) * TILE, :], preferred_element_type=F32)
-            total = total + jnp.where(lives[k, j] > 0, product, 0.0)
-        for n in range(len(parts)):
+            finish_tile(copies[k, j], lives[k, j], target(k, j))
+        total = jnp.dot(held[k], strip[...], preferred_element_type=F32)
+        for n in range(PARTS):
             piece = total[:, n * KW:(n + 1) * KW]
             if k % 2:
                 outs[3 * n + 2][k // 2] = piece
@@ -91,32 +99,30 @@
                 outs[3 * n + k // 2][...] = piece
 
 
-def forward(parts, places, count, tiles, sketch):
-    width = len(parts) * KW
+def forward(places, count, tiles, sketch):
     outs = call(
-        functools.partial(forward_body, parts),
-        [((TILE, KW), F32), ((TILE, KW), F32), ((2, TILE, KW), F32)] * len(parts), [SMEM, SMEM, HBM, HBM],
+        forward_body, [((TILE, KW), F32), ((TILE, KW), F32), ((2, TILE, KW), F32)] * PARTS, [SMEM, SMEM, HBM, HBM],
         (places, count, tiles, sketch),
         scratch=[
-            pltpu.VMEM((8, TILE, TILE), BF16), pltpu.VMEM((2 * TILE, width), BF16), pltpu.SemaphoreType.DMA((9,)),
+            pltpu.VMEM((4, TILE, 2 * TILE), BF16), pltpu.VMEM((2 * TILE, K), BF16), pltpu.SemaphoreType.DMA((9,)),
         ],
-        limit=20,
-    )
-    return [outs[3 * n:3 * n + 3] for n in range(len(parts))]
+        limit=24,
+    )
+    return [outs[3 * n:3 * n + 3] for n in range(PARTS)]
 
 
 def backward_body(places, count, tiles, i0, i1, i2, i3, out, held, sems):
-    images = (i0, i1, i2, i3)
     order = [(k, j) for j in range(2) for k in range(4)]
-    copies, lives = start_tiles(order, places, count, tiles, held, sems)
+
+    def target(k, j):
+        return held.at[j, pl.ds(k * TILE, TILE), :]
+
+    copies, lives = start_tiles(order, places, count, tiles, target, sems)
+    image = jnp.concatenate([i0[...], i1[...], i2[...], i3[...]], axis=0)
     for j in range(2):
-        part = jnp.zeros((TILE, KW), F32)
         for k in range(4):
-            copies[k, j].wait()
-            product = lax.dot_general(
-                held[order.index((k, j))], images[k][...], (((0,), (0,)), ((), ())), preferred_element_type=F32
-            )
-            part = part + jnp.where(lives[k, j] > 0, product, 0.0)
+            finish_tile(copies[k, j], lives[k, j], target(k, j))
+        part = lax.dot_general(held[j], image, (((0,), (0,)), ((), ())), preferred_element_type=F32)
         for y in range(2):
             for z in range(4):
                 for x in range(4):
@@ -127,20 +133,29 @@
 def backward(places, count, tiles, images):
     return call(
         backward_body, [((16, 64, KW), F32)], [SMEM, SMEM, HBM] + [VMEM] * 4, (places, count, tiles, *images),
-        scratch=[pltpu.VMEM((8, TILE, TILE), BF16), pltpu.SemaphoreType.DMA((8,))],
-        limit=20,
+        scratch=[pltpu.VMEM((2, 4 * TILE, TILE), BF16), pltpu.SemaphoreType.DMA((8,))],
+        limit=24, flops=16 * TILE * TILE * KW, moved=8 << 20,
     )[0]
 
 
-def join_body(s0, s1, s2, last, out):
-    for n, held in enumerate((s0, s1, s2)):
-        for z in range(4):
-            out[z, :, n * KW:(n + 1) * KW] = held[z * 16:(z + 1) * 16, :]
+def sum16(held, rows):
+    total = held[0, rows, :]
+    for p in range(1, 16):
+        total = total + held[p, rows, :]
+    return total
+
+
+def first_body(held, out):
     for z in range(4):
-        total = last[0, z * 16:(z + 1) * 16, :]
-        for p in range(1, 16):
-            total = total + last[p, z * 16:(z + 1) * 16, :]
-        out[z, :, 3 * KW:] = total
+        rows = slice(z * 16, (z + 1) * 16)
+        out[rows, :] = sum16(held, rows)
+
+
+def join_body(first, last, out):
+    for z in range(4):
+        rows = slice(z * 16, (z + 1) * 16)
+        out[z, :, :KW] = first[rows, :]
+        out[z, :, KW:] = sum16(last, rows)
 
 
 WIDE = 5 * NB
@@ -287,29 +302,19 @@
         owns.append(part[0] + got[0])
         others.append(part[1] + got[1])
 
-    for part in forward(list(range(PARTS)), places, tile_counts, tiles, strips):
+    for part in forward(places, tile_counts, tiles, strips):
         pair(part)
-    images, crossed = [], []
+    images = []
     for q in range(PARTS):
-        got = swap(others[q] if q < 2 else after(others[q], images[q - 2]), 2)
-        if q == 0:
-            got, others[1] = lax.optimization_barrier((got, others[1]))
-        images.append((owns[q] + got).astype(BF16))
-    for q in range(PARTS):
-        crossed.append(swap(images[q], 2))
-    summed = []
-    for q, image in enumerate(images):
-        across = crossed[q]
-        if q < PARTS - 1:
-            across, images[q + 1] = lax.optimization_barrier((across, images[q + 1]))
-        four = (image, swap(image, 1), across, swap(across, 1))
-        part = backward(places, tile_counts, tiles, four)
-        if q == PARTS - 1:
-            part, sketch_rows, *summed = lax.optimization_barrier((part, sketch_rows, *summed))
-            summed.append(trade(part, PLANES))
-        else:
-            summed.append(jnp.sum(trade(part, PLANES), axis=0))
-    joined = call(join_body, [((4, 16, K), F32)], [VMEM] * 4, summed, limit=16, moved=2 << 20)[0]
+        image = (owns[q] + swap(others[q], 2)).astype(BF16)
+        across, beside = swap(image, 2), swap(image, 1)
+        across, *others = lax.optimization_barrier((across, *others))
+        images.append((image, beside, across, swap(across, 1)))
+    first = backward(places, tile_counts, tiles, images[0])
+    first = call(first_body, [((64, KW), F32)], [VMEM], (trade(first, PLANES),), limit=16)[0]
+    last = backward(places, tile_counts, tiles, images[1])
+    last, first, sketch_rows = lax.optimization_barrier((last, first, sketch_rows))
+    joined = call(join_body, [((4, 16, K), F32)], [VMEM] * 2, (first, trade(last, PLANES)), limit=16)[0]
     shifted, spread = call(
         finish_body, [((16, K), F32), ((16, 16, WIDE), F32)], [VMEM] * 2, (trade(joined, COLUMNS), sketch_rows),
         limit=16, moved=1 << 20,

time: 297 us -> 288 us (0.970)
  starting transfers between devices: 54.4 us -> 34 us
  waiting for transfers between devices: 58 us -> 75.2 us
  Pallas kernels: 100 us -> 87 us
  blocking collectives: 71.1 us -> 79.8 us
  other arithmetic: 8.6 us -> 2.99 us
  local copies, waits for them, and re-layouts: 2.48 us -> 5.77 us
    ppermute x23 -> x13, waiting for transfers between devices: 50 us -> 69.4 us  [swap(): return lax.ppermute(value, 'col', [(c, c ^ bit) for c in range(4)])]
    all_to_all x3 -> x1, starting transfers between devices: 19.5 us -> 5.58 us  [trade(): lax.all_to_all(value, 'row', 0, 0, tiled=True, axis_index_groups=groups)]
    pallas_call x9 -> x8, Pallas kernels: 100 us -> 87 us  [call(): pl.pallas_call(body, out_shape=tuple((jax.ShapeDtypeStruct(shape, dtype)...]
    all_to_all x4, blocking collectives: 71.1 us -> 79.8 us  [trade(): lax.all_to_all(value, 'row', 0, 0, tiled=True, axis_index_groups=groups)]
    ppermute x23 -> x13, starting transfers between devices: 30.3 us -> 22.6 us  [swap(): return lax.ppermute(value, 'col', [(c, c ^ bit) for c in range(4)])]
    unnamed x4 -> x10, local copies, waits for them, and re-layouts: 0.85 us -> 4.14 us
  transfers between devices with their start and end apart: 28 -> 16, of which waited for: 16 -> 12; matrix products, arithmetic and copies ran while one was open for 3% -> 1% of each run, Pallas kernels for 8% -> 4%
where the time goes in v3:
time: 288 us; the launch traced here: 286 us
  Pallas kernels  87 us (30%)
  blocking collectives  79.8 us (28%)
  waiting for transfers between devices  75.2 us (26%)
  starting transfers between devices  34 us (12%)
  local copies, waits for them, and re-layouts  5.77 us (2%)
  other arithmetic  2.99 us (1%)
    pallas_call x8, Pallas kernels, call(): pl.pallas_call(body, out_shape=tuple((jax.ShapeDtypeStruct(shape, dtype)...  87 us
    all_to_all x4, blocking collectives, trade(): lax.all_to_all(value, 'row', 0, 0, tiled=True, axis_index_groups=groups)  79.8 us
    ppermute x13, waiting for transfers between devices, swap(): return lax.ppermute(value, 'col', [(c, c ^ bit) for c in range(4)])  69.4 us
    ppermute x13, starting transfers between devices, swap(): return lax.ppermute(value, 'col', [(c, c ^ bit) for c in range(4)])  22.6 us
    ppermute x2, starting transfers between devices, swap_level(): return lax.ppermute(value, 'row', [(r, r ^ bit * 4) for r in range(64)])  5.87 us
    ppermute x2, waiting for transfers between devices, swap_level(): return lax.ppermute(value, 'row', [(r, r ^ bit * 4) for r in range(64)])  5.8 us
  transfers between devices with their start and end apart: 16, of which 12 were waited for; matrix products, arithmetic and copies ran while one was open for 1% of the time, Pallas kernels for 4%

profile of v3, /device:TPU:1, one launch (start us, length us, event | category | flops | bytes accessed | tf_op | source)
XLA Modules:
  0.0 286.3 jit_solution(1694287040258109326)
XLA Ops:
  0.6 0.8 copy.7.places
  2.0 7.7 %shard_map.59 = (f32[512,512]{1,0:T(8,128)S(1)}, f32[512,512]{1,0:T(8,128)S(1)}, f32[2,512,512]{2,1,0:T(8,128)S(1)}, f32[512,512]{1,0:T(8,128)S(1)}, f32[512,512]{1,0:T(8,128)S(1)}, /*index=5*/f32[2,512,512]{2,1,0:T(8,128)S(1)}) custom-call(s32[8,2]{1,0:T(8,128)S(1)} %copy.7.places, s32[1,1]{1,0:T(1,128)S(6)} %copy.9.count, bf16[8,512,512]{2,1,0:T(8,128)(2,1)} %bitcast.27, ...), custom_call_target="tpu_custom_call" | custom-call | tf_op jit(solution)/shard_map/pallas_call | solution.py:26
  9.8 3.2 %collective-permute-start.1 = (f32[2,512,512]{2,1,0:T(8,128)S(1)}, f32[2,512,512]{2,1,0:T(8,128)S(1)}, u32[]{:S(2)}, u32[]{:S(2)}) collective-permute-start(f32[2,512,512]{2,1,0:T(8,128)S(1)} %get-tuple-element.23), channel_id=1, source_target_pairs={{0,1},{1,0},{2,3},{3,2},{4,5},{5,4},{6,7},{7,6},{8,9},{9,8},{10,11... | collective-permute-start | bytes 6291464 | tf_op jit(solution)/shard_map/ppermute | solution.py:46
  13.0 0.1 collective-permute-start
  13.1 3.7 %collective-permute-done.1 = f32[2,512,512]{2,1,0:T(8,128)S(1)} collective-permute-done((f32[2,512,512]{2,1,0:T(8,128)S(1)}, f32[2,512,512]{2,1,0:T(8,128)S(1)}, u32[]{:S(2)}, u32[]{:S(2)}) %collective-permute-start.1) | collective-permute-done | bytes 2097184 | tf_op jit(solution)/shard_map/ppermute | solution.py:46
  16.8 0.2 fusion.1
  17.0 0.1 collective-permute-start.2
  17.1 24.3 %collective-permute-done.2 = f32[512,512]{1,0:T(8,128)S(1)} collective-permute-done((f32[512,512]{1,0:T(8,128)S(1)}, f32[512,512]{1,0:T(8,128)S(1)}, u32[]{:S(2)}, u32[]{:S(2)}) %collective-permute-start.2) | collective-permute-done | bytes 1048608 | tf_op jit(solution)/shard_map/ppermute | solution.py:46
  41.4 0.4 fusion.4.i0
  41.9 0.1 collective-permute-start.3
  42.0 0.2 fusion
  42.2 1.6 collective-permute-start.8
  43.8 10.4 %collective-permute-done.3.i2 = bf16[512,512]{1,0:T(8,128)(2,1)S(1)} collective-permute-done((bf16[512,512]{1,0:T(8,128)(2,1)S(1)}, bf16[512,512]{1,0:T(8,128)(2,1)S(1)}, u32[]{:S(2)}, u32[]{:S(2)}) %collective-permute-start.3) | collective-permute-done | bytes 524320 | tf_op jit(solution)/shard_map/ppermute | solution.py:46
  54.2 2.1 collective-permute-start.9
  56.3 1.5 collective-permute-done.9.i3
  57.8 5.3 %shard_map.61 = f32[16,64,512]{2,1,0:T(8,128)S(1)} custom-call(s32[8,2]{1,0:T(8,128)S(1)} %copy.7.places, s32[1,1]{1,0:T(1,128)S(6)} %copy.9.count, bf16[8,512,512]{2,1,0:T(8,128)(2,1)} %bitcast.28, bf16[512,512]{1,0:T(8,128)(2,1)S(1)} %fusion.4.i0, bf16[512,512]{1,0:T(8,128)(2,1)S(1)} %collective-permute-done.8.i1, ...), custom_call_target="tpu_custom_call" | custom-call | flops 2147483648 | bytes 8388608 | tf_op jit(solution)/shard_map/pallas_call | solution.py:26
  63.2 1.3 copy-done
  64.5 5.6 %all-to-all-start = ((f32[16,64,512]{2,1,0:T(8,128)}), f32[16,64,512]{2,1,0:T(8,128)S(1)}, u32[]{:S(2)}, u32[]{:S(2)}) async-start(f32[16,64,512]{2,1,0:T(8,128)} %copy-done), calls=%async_computation | async-start | bytes 4194304 | tf_op jit(solution)/shard_map/all_to_all | solution.py:42
  70.1 11.1 %collective-permute-done.4 = f32[512,512]{1,0:T(8,128)} collective-permute-done((f32[512,512]{1,0:T(8,128)S(1)}, f32[512,512]{1,0:T(8,128)}, u32[]{:S(2)}, u32[]{:S(2)}) %collective-permute-start.4) | collective-permute-done | bytes 1048608 | tf_op jit(solution)/shard_map/ppermute | solution.py:46
  81.2 2.1 fusion.7.i0
  83.3 0.1 collective-permute-start.6
  83.4 1.1 collective-permute-start.5
  84.5 11.6 %collective-permute-done.6.i2 = bf16[512,512]{1,0:T(8,128)(2,1)S(1)} collective-permute-done((bf16[512,512]{1,0:T(8,128)(2,1)S(1)}, bf16[512,512]{1,0:T(8,128)(2,1)S(1)}, u32[]{:S(2)}, u32[]{:S(2)}) %collective-permute-start.6) | collective-permute-done | bytes 524320 | tf_op jit(solution)/shard_map/ppermute | solution.py:46
  96.1 1.7 collective-permute-start.7
  97.7 0.8 constant_dynamic-slice_fusion.sketch_rows
  98.5 0.9 collective-permute-done.7.i3
  99.4 5.9 %shard_map.60 = f32[16,64,512]{2,1,0:T(8,128)S(1)} custom-call(s32[8,2]{1,0:T(8,128)S(1)} %copy.7.places, s32[1,1]{1,0:T(1,128)S(6)} %copy.9.count, bf16[8,512,512]{2,1,0:T(8,128)(2,1)} %bitcast.29, bf16[512,512]{1,0:T(8,128)(2,1)S(1)} %fusion.7.i0, bf16[512,512]{1,0:T(8,128)(2,1)} %collective-permute-done.5.i1, ...), custom_call_target="tpu_custom_call" | custom-call | flops 2147483648 | bytes 8388608 | tf_op jit(solution)/shard_map/pallas_call | solution.py:26
  105.4 1.3 copy-done.1
  106.7 0.1 shard_map.62.first
  106.8 1.5 copy-done.2
  108.3 33.5 %all_to_all.25.last = f32[16,64,512]{2,1,0:T(8,128)S(1)} all-to-all(f32[16,64,512]{2,1,0:T(8,128)S(1)} %copy-done.2), channel_id=1, replica_groups={{0,4,8,12,64,68,72,76,128,132,136,140,192,196,200,204},{16,20,24,28,80,..., dimensions={0} | all-to-all | bytes 4194304 | tf_op jit(solution)/shard_map/all_to_all | solution.py:42
  141.7 0.1 shard_map.63
  141.9 15.6 %all_to_all.26.got = f32[4,16,1024]{2,1,0:T(8,128)S(1)} all-to-all(f32[4,16,1024]{2,1,0:T(8,128)S(1)} %shard_map.63), channel_id=1, replica_groups={{0,16,32,48},{4,20,36,52},{8,24,40,56},{12,28,44,60},{64,80,96,112},{68..., dimensions={0} | all-to-all | bytes 524288 | tf_op jit(solution)/shard_map/all_to_all | solution.py:42
  157.6 12.7 %all_to_all.27.rows_in = f32[16,16,640]{2,1,0:T(8,128)S(1)} all-to-all(f32[16,16,640]{2,1,0:T(8,128)S(1)} %get-tuple-element.32), channel_id=1, replica_groups={{0,4,8,12,64,68,72,76,128,132,136,140,192,196,200,204},{16,20,24,28,80,..., dimensions={0} | all-to-all | bytes 1310720 | tf_op jit(solution)/shard_map/all_to_all | solution.py:42
  170.2 0.5 shard_map.65
  170.8 5.2 %collective-permute-start.10 = (f32[32,640]{1,0:T(8,128)S(1)}, f32[32,640]{1,0:T(8,128)S(1)}, u32[]{:S(2)}, u32[]{:S(2)}) collective-permute-start(f32[32,640]{1,0:T(8,128)S(1)} %get-tuple-element.34), channel_id=1, source_target_pairs={{0,1},{1,0},{2,3},{3,2},{4,5},{5,4},{6,7},{7,6},{8,9},{9,8},{10,11... | collective-permute-start | bytes 245768 | tf_op jit(solution)/shard_map/ppermute | solution.py:46
  175.9 0.9 collective-permute-done.10
  176.9 1.4 collective-permute-start.11
  178.3 2.3 collective-permute-done.11
  180.6 1.5 collective-permute-start.12
  182.2 2.8 collective-permute-done.12
  184.9 4.4 %collective-permute-start.13 = (f32[32,640]{1,0:T(8,128)S(1)}, f32[32,640]{1,0:T(8,128)S(1)}, u32[]{:S(2)}, u32[]{:S(2)}) collective-permute-start(f32[32,640]{1,0:T(8,128)S(1)} %add.42), channel_id=1, source_target_pairs={{0,32},{4,36},{8,40},{12,44},{16,48},{20,52},{24,56},{28,60},{32,0... | collective-permute-start | bytes 245768 | tf_op jit(solution)/shard_map/ppermute | solution.py:50
  189.3 3.0 %collective-permute-done.13 = f32[32,640]{1,0:T(8,128)S(1)} collective-permute-done((f32[32,640]{1,0:T(8,128)S(1)}, f32[32,640]{1,0:T(8,128)S(1)}, u32[]{:S(2)}, u32[]{:S(2)}) %collective-permute-start.13) | collective-permute-done | bytes 81952 | tf_op jit(solution)/shard_map/ppermute | solution.py:50
  192.3 0.1 broadcast_in_dim.4
  192.5 18.1 %all_to_all.28.own = f32[16,32,640]{2,1,0:T(8,128)S(1)} all-to-all(f32[16,32,640]{2,1,0:T(8,128)S(1)} %broadcast_in_dim.4), channel_id=1, replica_groups={{0,4,8,12,64,68,72,76,128,132,136,140,192,196,200,204},{16,20,24,28,80,..., dimensions={0} | all-to-all | bytes 2621440 | tf_op jit(solution)/shard_map/all_to_all | solution.py:42
  210.5 5.8 %collective-permute-start.14 = (f32[16,32,640]{2,1,0:T(8,128)S(1)}, f32[16,32,640]{2,1,0:T(8,128)S(1)}, u32[]{:S(2)}, u32[]{:S(2)}) collective-permute-start(f32[16,32,640]{2,1,0:T(8,128)S(1)} %all_to_all.28.own), channel_id=1, source_target_pairs={{0,1},{1,0},{2,3},{3,2},{4,5},{5,4},{6,7},{7,6},{8,9},{9,8},{10,11... | collective-permute-start | bytes 3932168 | tf_op jit(solution)/shard_map/ppermute | solution.py:46
  216.4 2.7 collective-permute-done.14.other
  219.0 67.2 %shard_map.66 = (f32[16,1024]{1,0:T(8,128)}, f32[1024,1024]{1,0:T(8,128)}) custom-call(f32[16,32,640]{2,1,0:T(8,128)S(1)} %all_to_all.28.own, f32[16,32,640]{2,1,0:T(8,128)S(1)} %collective-permute-done.14.other, f32[16,1024]{1,0:T(8,128)S(1)} %get-tuple-element.35.shifted), custom_call_target="tpu_custom_call" | custom-call | flops 4294967296 | bytes 8388608 | tf_op jit(solution)/shard_map/pallas_call | solution.py:26
  (17 shorter events, 0.2 us)
Async XLA Ops:
  9.7 32.1 %copy-start.3 = (f32[512,512]{1,0:T(8,128)}, f32[512,512]{1,0:T(8,128)S(1)}, u32[]{:S(2)}) copy-start(f32[512,512]{1,0:T(8,128)S(1)} %get-tuple-element.20) | copy-start | bytes 3145732
  9.8 7.0 %collective-permute-start.1 = (f32[2,512,512]{2,1,0:T(8,128)S(1)}, f32[2,512,512]{2,1,0:T(8,128)S(1)}, u32[]{:S(2)}, u32[]{:S(2)}) collective-permute-start(f32[2,512,512]{2,1,0:T(8,128)S(1)} %get-tuple-element.23), channel_id=1, source_target_pairs={{0,1},{1,0},{2,3},{3,2},{4,5},{5,4},{6,7},{7,6},{8,9},{9,8},{10,11... | collective-permute-start | bytes 6291464 | tf_op jit(solution)/shard_map/ppermute | solution.py:46
  13.0 29.0 %collective-permute-start = (f32[2,512,512]{2,1,0:T(8,128)S(1)}, f32[2,512,512]{2,1,0:T(8,128)S(1)}, u32[]{:S(2)}, u32[]{:S(2)}) collective-permute-start(f32[2,512,512]{2,1,0:T(8,128)S(1)} %get-tuple-element.21), channel_id=1, source_target_pairs={{0,1},{1,0},{2,3},{3,2},{4,5},{5,4},{6,7},{7,6},{8,9},{9,8},{10,11... | collective-permute-start | bytes 6291464 | tf_op jit(solution)/shard_map/ppermute | solution.py:46
  17.0 24.5 %collective-permute-start.2 = (f32[512,512]{1,0:T(8,128)S(1)}, f32[512,512]{1,0:T(8,128)S(1)}, u32[]{:S(2)}, u32[]{:S(2)}) collective-permute-start(f32[512,512]{1,0:T(8,128)S(1)} %fusion.1), channel_id=1, source_target_pairs={{0,2},{1,3},{2,0},{3,1},{4,6},{5,7},{6,4},{7,5},{8,10},{9,11},{10,... | collective-permute-start | bytes 3145736 | tf_op jit(solution)/shard_map/ppermute | solution.py:46
  41.9 12.3 %collective-permute-start.3 = (bf16[512,512]{1,0:T(8,128)(2,1)S(1)}, bf16[512,512]{1,0:T(8,128)(2,1)S(1)}, u32[]{:S(2)}, u32[]{:S(2)}) collective-permute-start(bf16[512,512]{1,0:T(8,128)(2,1)S(1)} %fusion.4.i0), channel_id=1, source_target_pairs={{0,2},{1,3},{2,0},{3,1},{4,6},{5,7},{6,4},{7,5},{8,10},{9,11},{10,... | collective-permute-start | bytes 1572872 | tf_op jit(solution)/shard_map/ppermute | solution.py:46
  42.0 14.3 %copy-start.4 = (f32[2,512,512]{2,1,0:T(8,128)}, f32[2,512,512]{2,1,0:T(8,128)S(1)}, u32[]{:S(2)}) copy-start(f32[2,512,512]{2,1,0:T(8,128)S(1)} %collective-permute-done) | copy-start | bytes 6291460
  42.2 14.1 %collective-permute-start.8 = (bf16[512,512]{1,0:T(8,128)(2,1)S(1)}, bf16[512,512]{1,0:T(8,128)(2,1)S(1)}, u32[]{:S(2)}, u32[]{:S(2)}) collective-permute-start(bf16[512,512]{1,0:T(8,128)(2,1)S(1)} %fusion.4.i0), channel_id=1, source_target_pairs={{0,1},{1,0},{2,3},{3,2},{4,5},{5,4},{6,7},{7,6},{8,9},{9,8},{10,11... | collective-permute-start | bytes 1572872 | tf_op jit(solution)/shard_map/ppermute | solution.py:46
  54.2 3.7 %collective-permute-start.9 = (bf16[512,512]{1,0:T(8,128)(2,1)S(1)}, bf16[512,512]{1,0:T(8,128)(2,1)S(1)}, u32[]{:S(2)}, u32[]{:S(2)}) collective-permute-start(bf16[512,512]{1,0:T(8,128)(2,1)S(1)} %collective-permute-done.3.i2), channel_id=1, source_target_pairs={{0,1},{1,0},{2,3},{3,2},{4,5},{5,4},{6,7},{7,6},{8,9},{9,8},{10,11... | collective-permute-start | bytes 1572872 | tf_op jit(solution)/shard_map/ppermute | solution.py:46
  56.3 24.9 %collective-permute-start.4 = (f32[512,512]{1,0:T(8,128)S(1)}, f32[512,512]{1,0:T(8,128)}, u32[]{:S(2)}, u32[]{:S(2)}) collective-permute-start(f32[512,512]{1,0:T(8,128)S(1)} %fusion), channel_id=1, source_target_pairs={{0,2},{1,3},{2,0},{3,1},{4,6},{5,7},{6,4},{7,5},{8,10},{9,11},{10,... | collective-permute-start | bytes 3145736 | tf_op jit(solution)/shard_map/ppermute | solution.py:46
  63.1 1.3 copy-start
  64.5 42.2 %all-to-all-start = ((f32[16,64,512]{2,1,0:T(8,128)}), f32[16,64,512]{2,1,0:T(8,128)S(1)}, u32[]{:S(2)}, u32[]{:S(2)}) async-start(f32[16,64,512]{2,1,0:T(8,128)} %copy-done), calls=%async_computation | async-start | bytes 4194304 | tf_op jit(solution)/shard_map/all_to_all | solution.py:42
  83.3 12.8 %collective-permute-start.6 = (bf16[512,512]{1,0:T(8,128)(2,1)S(1)}, bf16[512,512]{1,0:T(8,128)(2,1)S(1)}, u32[]{:S(2)}, u32[]{:S(2)}) collective-permute-start(bf16[512,512]{1,0:T(8,128)(2,1)S(1)} %fusion.7.i0), channel_id=1, source_target_pairs={{0,2},{1,3},{2,0},{3,1},{4,6},{5,7},{6,4},{7,5},{8,10},{9,11},{10,... | collective-permute-start | bytes 1572872 | tf_op jit(solution)/shard_map/ppermute | solution.py:46
  83.4 15.1 %collective-permute-start.5 = (bf16[512,512]{1,0:T(8,128)(2,1)S(1)}, bf16[512,512]{1,0:T(8,128)(2,1)}, u32[]{:S(2)}, u32[]{:S(2)}) collective-permute-start(bf16[512,512]{1,0:T(8,128)(2,1)S(1)} %fusion.7.i0), channel_id=1, source_target_pairs={{0,1},{1,0},{2,3},{3,2},{4,5},{5,4},{6,7},{7,6},{8,9},{9,8},{10,11... | collective-permute-start | bytes 1572872 | tf_op jit(solution)/shard_map/ppermute | solution.py:46
  96.1 3.3 %collective-permute-start.7 = (bf16[512,512]{1,0:T(8,128)(2,1)S(1)}, bf16[512,512]{1,0:T(8,128)(2,1)}, u32[]{:S(2)}, u32[]{:S(2)}) collective-permute-start(bf16[512,512]{1,0:T(8,128)(2,1)S(1)} %collective-permute-done.6.i2), channel_id=1, source_target_pairs={{0,1},{1,0},{2,3},{3,2},{4,5},{5,4},{6,7},{7,6},{8,9},{9,8},{10,11... | collective-permute-start | bytes 1572872 | tf_op jit(solution)/shard_map/ppermute | solution.py:46
  105.3 1.3 copy-start.1
  106.7 1.6 copy-start.2
  170.8 6.1 %collective-permute-start.10 = (f32[32,640]{1,0:T(8,128)S(1)}, f32[32,640]{1,0:T(8,128)S(1)}, u32[]{:S(2)}, u32[]{:S(2)}) collective-permute-start(f32[32,640]{1,0:T(8,128)S(1)} %get-tuple-element.34), channel_id=1, source_target_pairs={{0,1},{1,0},{2,3},{3,2},{4,5},{5,4},{6,7},{7,6},{8,9},{9,8},{10,11... | collective-permute-start | bytes 245768 | tf_op jit(solution)/shard_map/ppermute | solution.py:46
  176.9 3.8 %collective-permute-start.11 = (f32[32,640]{1,0:T(8,128)S(1)}, f32[32,640]{1,0:T(8,128)S(1)}, u32[]{:S(2)}, u32[]{:S(2)}) collective-permute-start(f32[32,640]{1,0:T(8,128)S(1)} %add.40), channel_id=1, source_target_pairs={{0,2},{1,3},{2,0},{3,1},{4,6},{5,7},{6,4},{7,5},{8,10},{9,11},{10,... | collective-permute-start | bytes 245768 | tf_op jit(solution)/shard_map/ppermute | solution.py:46
  180.6 4.3 %collective-permute-start.12 = (f32[32,640]{1,0:T(8,128)S(1)}, f32[32,640]{1,0:T(8,128)S(1)}, u32[]{:S(2)}, u32[]{:S(2)}) collective-permute-start(f32[32,640]{1,0:T(8,128)S(1)} %add.41), channel_id=1, source_target_pairs={{0,16},{4,20},{8,24},{12,28},{16,0},{20,4},{24,8},{28,12},{32,48},... | collective-permute-start | bytes 245768 | tf_op jit(solution)/shard_map/ppermute | solution.py:50
  184.9 7.4 %collective-permute-start.13 = (f32[32,640]{1,0:T(8,128)S(1)}, f32[32,640]{1,0:T(8,128)S(1)}, u32[]{:S(2)}, u32[]{:S(2)}) collective-permute-start(f32[32,640]{1,0:T(8,128)S(1)} %add.42), channel_id=1, source_target_pairs={{0,32},{4,36},{8,40},{12,44},{16,48},{20,52},{24,56},{28,60},{32,0... | collective-permute-start | bytes 245768 | tf_op jit(solution)/shard_map/ppermute | solution.py:50
  210.5 8.5 %collective-permute-start.14 = (f32[16,32,640]{2,1,0:T(8,128)S(1)}, f32[16,32,640]{2,1,0:T(8,128)S(1)}, u32[]{:S(2)}, u32[]{:S(2)}) collective-permute-start(f32[16,32,640]{2,1,0:T(8,128)S(1)} %all_to_all.28.own), channel_id=1, source_target_pairs={{0,1},{1,0},{2,3},{3,2},{4,5},{5,4},{6,7},{7,6},{8,9},{9,8},{10,11... | collective-permute-start | bytes 3932168 | tf_op jit(solution)/shard_map/ppermute | solution.py:46
